TPU v7x, 32 devices: a whole 2x2x4 slice. The times are simulated.
32 devices in a mesh: grp: 2 (over y), freq: 4 (over z), shot: 2 (over x), rcv: 2 (over core).
Axes of the slice: x: 2, y: 2, z: 4, core: 2. Of those that a mesh axis runs over, the one named last changes fastest.
Arguments:
- data: bfloat16 [2, 256, 32, 4096], P(None, 'freq', ('grp', 'shot'), 'rcv'), parts along dimension 2, may hold values from -6 to 6
- estimate: bfloat16 [2, 256, 32, 4096], P(None, 'freq', ('grp', 'shot'), 'rcv'), parts along dimension 2, may hold values from -0.09375 to 0.09375
- window_data: bfloat16 [2, 256, 32, 16], P(None, 'freq', ('grp', 'shot')), parts along dimension 2, may hold values from -6 to 6
- wavelet: float32 [2, 512], P(None, ('grp', 'freq')), parts along dimension 1, may hold values from -24 to 24
- positions: int32 [32], P(('grp', 'shot')), parts along dimension 0, may hold values from 0 to 4095
- bins: int32 [512], P('grp'), parts along dimension 0, may hold values from 0 to 399
- threshold: int32 [2], P('grp'), parts along dimension 0, may hold values from 8 to 40
- step: float32 [2], P('grp'), parts along dimension 0, may hold values from 0.25 to 1
Outputs:
- primaries: bfloat16 [1024, 32, 4096], P('freq', ('grp', 'shot'), 'rcv'), parts along dimension 1
There are 2 independent parts, one for each index of `grp`. A program takes and returns all parts, laid end to end along the dimension named above; each array names one. Nothing has to cross between parts.
All inputs are finite; a program needn't handle non-finite values.
Results may differ from a plain program's by a relative error of at most 0.0059.
The roundings to bfloat16 on the way count: a program that leaves them out, or rounds other values in their place, can miss the bound.
Values may be sent and summed in bfloat16 or wider, within the bound.
A program may use at most 64 MiB of HBM per device.

v0:
```python
from functools import partial
import math

import jax
import jax.numpy as jnp
from jax import lax
from jax.experimental import pallas as pl
from jax.experimental.pallas import tpu as pltpu
from jax.sharding import PartitionSpec as P

NF = 256
RCV = 4096
NT = 1024
FC = 8
BLOCK = 256
LAG = 1
MESH = pl.DeviceIdType.MESH


def iota(shape, dim):
    return lax.broadcasted_iota(jnp.int32, shape, dim)


def make_traces(u, table, lv, gain, rows, t_group, sparse, out):
    groups, _, width = u.shape
    part = 2 * FC
    nt = table.shape[0]
    for i in range(rows):
        ui = u[:, i * part:(i + 1) * part, :].reshape(groups * part, width)
        tr = jnp.dot(table[...], ui, preferred_element_type=jnp.float32) * gain
        sparse[i] = (jnp.maximum(tr - lv, 0.0) + jnp.minimum(tr + lv, 0.0)).astype(jnp.bfloat16)
    n = t_group * rows
    dst, src = iota((n, n), 0), iota((n, n), 1)
    perm = (src == (dst % rows) * t_group + dst // rows).astype(jnp.bfloat16)
    for g in range(nt // t_group):
        x = sparse[:, g * t_group:(g + 1) * t_group, :].reshape(n, width)
        out[g * n:(g + 1) * n, :] = jnp.dot(
            perm, x, preferred_element_type=jnp.float32
        ).astype(jnp.bfloat16)


def update_kernel(
    nx, nz, nchunk, rows, lines, norm, blocks, helped, gain, t_group,
    data, est, win, wav, pos, step, level, table, out, given,
    down, est_p, upd, mod_mine, mod_other, ubuf, sparse, made,
    x_send, x_recv, c_send, c_recv, za_send, za_recv, zb_send, zb_recv,
    zc_send, zc_recv, g_send, g_recv, own_sem, ubuf_sem,
):
    mx = lax.axis_index("shot")
    mz = lax.axis_index("freq")
    mc = lax.axis_index("rcv")
    width = data.shape[2]
    fl = FC * lines
    fi = FC * rows

    barrier = pltpu.get_barrier_semaphore()
    for d in range(1, nx):
        pl.semaphore_signal(
            barrier, inc=1, device_id={"shot": lax.rem(mx + d, nx)}, device_id_type=MESH
        )
    pl.semaphore_signal(barrier, inc=1, device_id={"rcv": 1 - mc}, device_id_type=MESH)

    @pl.when(mz > 0)
    def _():
        pl.semaphore_signal(barrier, inc=1, device_id={"freq": mz - 1}, device_id_type=MESH)

    @pl.when(mz < nz - 1)
    def _():
        pl.semaphore_signal(barrier, inc=1, device_id={"freq": mz + 1}, device_id_type=MESH)

    ends = (mz > 0).astype(jnp.int32) + (mz < nz - 1).astype(jnp.int32)
    pl.semaphore_wait(barrier, nx + ends)

    def x_copy(d, k):
        piece = down.at[k, :, pl.ds(mx * fl, fl)]
        return pltpu.make_async_remote_copy(
            src_ref=piece, dst_ref=piece,
            send_sem=x_send.at[d, k], recv_sem=x_recv.at[d, k],
            device_id={"shot": lax.rem(mx + d, nx)}, device_id_type=MESH,
        )

    def c_copy(k):
        return pltpu.make_async_remote_copy(
            src_ref=mod_mine.at[k], dst_ref=mod_other.at[k],
            send_sem=c_send.at[k], recv_sem=c_recv.at[k],
            device_id={"rcv": 1 - mc}, device_id_type=MESH,
        )

    def w_of(way):
        return 0 if way > 0 else 1

    def last(z, way):
        return z == (nz - 1 if way > 0 else 0)

    def a_copy(src, slot, k, way):
        return pltpu.make_async_remote_copy(
            src_ref=src, dst_ref=out.at[pl.ds(0, helped), slot, k],
            send_sem=za_send.at[w_of(way), slot, k], recv_sem=za_recv.at[w_of(way), slot, k],
            device_id={"freq": mz + way}, device_id_type=MESH,
        )

    def b_copy(src, slot, k, way):
        return pltpu.make_async_remote_copy(
            src_ref=src, dst_ref=out.at[pl.ds(helped, blocks - helped), slot, k],
            send_sem=zb_send.at[w_of(way), slot, k], recv_sem=zb_recv.at[w_of(way), slot, k],
            device_id={"freq": mz + way}, device_id_type=MESH,
        )

    def block_copy(slot, b, way):
        piece = out.at[b, slot]
        return pltpu.make_async_remote_copy(
            src_ref=piece, dst_ref=piece,
            send_sem=zc_send.at[w_of(way), slot, b], recv_sem=zc_recv.at[w_of(way), slot, b],
            device_id={"freq": mz + way}, device_id_type=MESH,
        )

    def given_copy(b, way):
        return pltpu.make_async_remote_copy(
            src_ref=made.at[b], dst_ref=given.at[b],
            send_sem=g_send.at[b], recv_sem=g_recv.at[b],
            device_id={"freq": mz + way}, device_id_type=MESH,
        )

    a_own = lambda k: upd.at[k, pl.ds(0, helped)]
    b_own = lambda k: upd.at[k, pl.ds(helped, blocks - helped)]
    a_out = lambda slot, k: out.at[pl.ds(0, helped), slot, k]
    b_out = lambda slot, k: out.at[pl.ds(helped, blocks - helped), slot, k]

    def own_copy(k):
        return pltpu.make_async_copy(upd.at[k], out.at[:, mz, k], own_sem.at[k])

    column = mc * width + iota((lines, width), 1)
    select = (column == pos[:, :]).astype(jnp.float32)

    def make_down(k, carry):
        for c in range(2):
            parts = []
            lines_k = data[c, pl.ds(pl.multiple_of(k * fl, fl), fl)].astype(jnp.float32)
            for f in range(FC):
                w = wav[c, k * FC + f]
                parts.append(w * select - lines_k[f * lines:(f + 1) * lines])
            down[k, c, pl.ds(pl.multiple_of(mx * fl, fl), fl)] = jnp.concatenate(
                parts, axis=0
            ).astype(jnp.bfloat16)
        for d in range(1, nx):
            x_copy(d, k).start()
        return carry

    lax.fori_loop(0, nchunk, make_down, 0)

    n = 2 * fi
    dst, src = iota((n, n), 0), iota((n, n), 1)
    want = (dst // FC % 2) * fi + (dst % FC) * rows + dst // (2 * FC)
    perm = (src == want).astype(jnp.bfloat16)

    def chunk_of(ref, k):
        part = pl.ds(pl.multiple_of(k * fi, fi), fi)
        return jnp.concatenate([ref[0, part], ref[1, part]], axis=0)

    def permute(k, carry):
        est_p[k] = jnp.dot(
            perm, chunk_of(est, k), preferred_element_type=jnp.float32
        ).astype(jnp.bfloat16)
        return carry

    lax.fori_loop(0, nchunk, permute, 0)

    cols = nx * fl
    shots = win.shape[2]
    s_row, s_col = iota((shots, cols), 0), iota((shots, cols), 1)
    spread = (s_row == (s_col // fl) * lines + s_col % lines).astype(jnp.bfloat16)
    shape3 = (rows, FC, cols)
    same = iota(shape3, 1) == iota(shape3, 2) % fl // lines
    scale = step[0]

    def model(k):
        for d in range(1, nx):
            here = down.at[k, :, pl.ds(lax.rem(mx + nx - d, nx) * fl, fl)]
            pltpu.make_async_remote_copy(
                src_ref=here, dst_ref=here,
                send_sem=x_send.at[d, k], recv_sem=x_recv.at[d, k],
                device_id={"shot": lax.rem(mx + d, nx)}, device_id_type=MESH,
            ).wait_recv()
        lines_k = down[k].reshape(2 * cols, width)
        m = lax.dot_general(
            est_p[k], lines_k, (((1,), (1,)), ((), ())), preferred_element_type=jnp.float32
        ).reshape(rows, 2, FC, 2 * cols)
        mod_mine[k, 0] = m[:, 0, :, :cols] - m[:, 1, :, cols:]
        mod_mine[k, 1] = m[:, 0, :, cols:] + m[:, 1, :, :cols]
        c_copy(k).start()

    def update(k):
        c_copy(k).wait_recv()
        total_re = mod_mine[k, 0] + mod_other[k, 0]
        total_im = mod_mine[k, 1] + mod_other[k, 1]
        w = jnp.dot(perm, chunk_of(win, k), preferred_element_type=jnp.float32).astype(jnp.bfloat16)
        w = jnp.dot(w, spread, preferred_element_type=jnp.float32).reshape(rows, 2, FC, cols)
        e_re = jnp.where(same, w[:, 0] - total_re, 0.0)
        e_im = jnp.where(same, w[:, 1] - total_im, 0.0)
        e = jnp.stack(
            [jnp.concatenate([e_re, e_im], axis=2), jnp.concatenate([e_im, -e_re], axis=2)], axis=1
        ).reshape(n, 2 * cols).astype(jnp.bfloat16)
        grad = jnp.dot(e, down[k].reshape(2 * cols, width), preferred_element_type=jnp.float32)
        new = (est_p[k].astype(jnp.float32) - scale * (grad * norm)).astype(jnp.bfloat16)
        for b in range(blocks):
            upd[k, b] = new[:, b * BLOCK:(b + 1) * BLOCK]
        own_copy(k).start()
        for way in (1, -1):
            @pl.when(jnp.logical_not(last(mz, way)))
            def _():
                b_copy(b_own(k), mz, k, way).start()

                if helped:
                    @pl.when(jnp.logical_not(last(mz + way, way)))
                    def _():
                        a_copy(a_own(k), mz, k, way).start()

    def near(k):
        for way in (1, -1):
            slot = mz - way

            @pl.when((slot >= 0) & (slot < nz))
            def _():
                b_copy(b_out(slot, k), slot, k, way).wait_recv()

                if helped:
                    @pl.when(jnp.logical_not(last(mz, way)))
                    def _():
                        a_copy(a_out(slot, k), slot, k, way).wait_recv()

                @pl.when(last(mz + way, way))
                def _():
                    b_copy(b_out(slot, k), slot, k, way).start()

    def step_of(k, carry):
        @pl.when(k < nchunk)
        def _():
            model(k)
            update(k)

        @pl.when(k >= LAG)
        def _():
            near(k - LAG)

        return carry

    lax.fori_loop(0, nchunk + LAG, step_of, 0)

    def own_done(k, carry):
        own_copy(k).wait()
        return carry

    lax.fori_loop(0, nchunk, own_done, 0)

    def hand_on(b, carry):
        for way in (1, -1):
            slot = mz - way
            inside = (slot >= 0) & (slot < nz)
            nxt = mz + way

            @pl.when(inside & (nxt > 0) & (nxt < nz - 1))
            def _():
                block_copy(slot, b, way).start()

        return carry

    lax.fori_loop(0, blocks, hand_on, 0)

    def far(h, carry):
        def one(b, carry):
            for way in (1, -1):
                slot = mz - way * h
                nxt = mz + way
                inside = (slot >= 0) & (slot < nz)
                at_end = last(mz, way)

                @pl.when(inside & jnp.logical_not(at_end))
                def _():
                    block_copy(slot, b, way).wait_recv()

                    @pl.when(jnp.logical_not(last(nxt, way)) | (b >= helped))
                    def _():
                        block_copy(slot, b, way).start()

                    if helped:
                        @pl.when(last(nxt, way) & (b < helped) & last(slot, -way))
                        def _():
                            load = pltpu.make_async_copy(out.at[b], ubuf, ubuf_sem)
                            load.start()
                            load.wait()
                            make_traces(
                                ubuf.reshape(nz * nchunk, ubuf.shape[2], BLOCK), table, level[0],
                                gain, rows, t_group, sparse, made.at[b],
                            )
                            given_copy(b, way).start()

                @pl.when(inside & at_end & (b >= helped))
                def _():
                    if not near_by:
                        block_copy(slot, b, way).wait_recv()

            return carry

        near_by = isinstance(h, int)
        return lax.fori_loop(0, blocks, one, carry)

    def end_chunk(k, carry):
        for way in (1, -1):
            slot = mz - 2 * way

            @pl.when((slot >= 0) & (slot < nz) & last(mz, way))
            def _():
                b_copy(b_out(slot, k), slot, k, way).wait_recv()

        return carry

    if nz > 2:
        lax.fori_loop(0, nchunk, end_chunk, 0)
        far(2, 0)
    lax.fori_loop(3, nz, far, 0)

    if helped:
        def take(b, carry):
            for way in (1, -1):
                @pl.when(last(mz, way))
                def _():
                    given_copy(b, way).wait_recv()

                @pl.when(last(mz + way, way))
                def _():
                    given_copy(b, way).wait_send()

            return carry

        lax.fori_loop(0, helped, take, 0)

    def drain(k, carry):
        for d in range(1, nx):
            x_copy(d, k).wait_send()
        c_copy(k).wait_send()
        for way in (1, -1):
            nxt = mz + way

            @pl.when(jnp.logical_not(last(mz, way)))
            def _():
                b_copy(b_own(k), mz, k, way).wait_send()

                if helped:
                    @pl.when(jnp.logical_not(last(nxt, way)))
                    def _():
                        a_copy(a_own(k), mz, k, way).wait_send()

            slot = mz - way

            @pl.when((slot >= 0) & (slot < nz) & last(nxt, way))
            def _():
                b_copy(b_own(k), slot, k, way).wait_send()

        return carry

    lax.fori_loop(0, nchunk, drain, 0)

    def drain_far(h, carry):
        def one(b, carry):
            for way in (1, -1):
                slot = mz - way * h
                nxt = mz + way
                inside = (slot >= 0) & (slot < nz) & (nxt >= 0) & (nxt < nz)
                to_end = last(nxt, way)

                @pl.when(inside & (jnp.logical_not(to_end) | ((b >= helped) & (h > 1))))
                def _():
                    block_copy(slot, b, way).wait_send()

            return carry

        return lax.fori_loop(0, blocks, one, carry)

    lax.fori_loop(1, nz, drain_far, 0)


def trace_kernel(rows, t_group, gain, helped, level, taken, table, u, given, out, sparse):
    ready = (pl.program_id(0) < helped) & (taken[0] > 0)

    @pl.when(ready)
    def _():
        out[...] = given[...]

    @pl.when(jnp.logical_not(ready))
    def _():
        make_traces(u, table, level[0], gain, rows, t_group, sparse, out)


def body(nx, nz, data, estimate, window_data, wavelet, positions, bins, threshold, step):
    _, nf, lines, width = data.shape
    rows = estimate.shape[2]
    shots = window_data.shape[3]
    nchunk = nf // FC
    norm = 1.0 / math.sqrt(shots * RCV)
    fi, cols = FC * rows, nx * FC * lines
    mz = lax.axis_index("freq")
    nt = NT // nz
    blocks, groups = width // BLOCK, nz * nchunk
    helped = 3 * blocks // 8 if nz >= 4 else 0
    held = max(helped, 1)
    gain, t_group = math.sqrt(RCV / NF), 32
    level = threshold.astype(jnp.float32) / 64.0

    def table_of(z):
        times = z * nt + lax.iota(jnp.int32, nt)
        phase = times[:, None] * bins[None, :] % NT
        angle = 2.0 * math.pi / NT * phase.astype(jnp.float32)
        table = jnp.stack([jnp.cos(angle), -jnp.sin(angle)], axis=1).astype(jnp.bfloat16)
        table = table.reshape(nt, 2, groups, FC).transpose(0, 2, 1, 3)
        return table.reshape(nt, 2 * nz * nf)

    vmem = pl.BlockSpec(memory_space=pltpu.VMEM)
    smem = pl.BlockSpec(memory_space=pltpu.SMEM)
    hbm = pl.BlockSpec(memory_space=pl.ANY)
    dma = pltpu.SemaphoreType.DMA
    spectra, given = pl.pallas_call(
        partial(
            update_kernel, nx, nz, nchunk, rows, lines, norm, blocks, helped, gain, t_group
        ),
        out_shape=(
            jax.ShapeDtypeStruct((blocks, nz, nchunk, 2 * fi, BLOCK), jnp.bfloat16),
            jax.ShapeDtypeStruct((held, nt * rows, BLOCK), jnp.bfloat16),
        ),
        in_specs=[vmem, vmem, vmem, smem, vmem, smem, smem, vmem],
        out_specs=(hbm, hbm),
        scratch_shapes=[
            pltpu.VMEM((nchunk, 2, cols, width), jnp.bfloat16),
            pltpu.VMEM((nchunk, 2 * fi, width), jnp.bfloat16),
            pltpu.VMEM((nchunk, blocks, 2 * fi, BLOCK), jnp.bfloat16),
            pltpu.VMEM((nchunk, 2, rows, FC, cols), jnp.float32),
            pltpu.VMEM((nchunk, 2, rows, FC, cols), jnp.float32),
            pltpu.VMEM((nz, nchunk, 2 * fi, BLOCK), jnp.bfloat16),
            pltpu.VMEM((rows, nt, BLOCK), jnp.bfloat16),
            pltpu.VMEM((held, nt * rows, BLOCK), jnp.bfloat16),
            dma((nx, nchunk)), dma((nx, nchunk)),
            dma((nchunk,)), dma((nchunk,)),
            dma((2, nz, nchunk)), dma((2, nz, nchunk)),
            dma((2, nz, nchunk)), dma((2, nz, nchunk)),
            dma((2, nz, blocks)), dma((2, nz, blocks)),
            dma((held,)), dma((held,)),
            dma((nchunk,)), dma,
        ],
        compiler_params=pltpu.CompilerParams(
            collective_id=0, has_side_effects=True, vmem_limit_bytes=58 << 20
        ),
        name="update",
    )(
        data.reshape(2, nf * lines, width),
        estimate.reshape(2, nf * rows, width),
        window_data.reshape(2, nf * rows, shots),
        wavelet,
        positions[:, None],
        step,
        level,
        table_of(jnp.where(mz < nz // 2, 0, nz - 1)),
    )
    taken = ((mz == 0) | (mz == nz - 1)).astype(jnp.int32)[None]
    traces = pl.pallas_call(
        partial(trace_kernel, rows, t_group, gain, helped),
        out_shape=jax.ShapeDtypeStruct((nt * rows, width), jnp.bfloat16),
        grid=(blocks,),
        in_specs=[
            smem,
            smem,
            pl.BlockSpec((nt, 2 * nz * nf), lambda j: (0, 0)),
            pl.BlockSpec((None, groups, 2 * fi, BLOCK), lambda j: (j, 0, 0, 0)),
            pl.BlockSpec(
                (None, nt * rows, BLOCK), lambda j: (jnp.minimum(j, held - 1), 0, 0)
            ),
        ],
        out_specs=pl.BlockSpec((nt * rows, BLOCK), lambda j: (0, j)),
        scratch_shapes=[pltpu.VMEM((rows, nt, BLOCK), jnp.bfloat16)],
        compiler_params=pltpu.CompilerParams(vmem_limit_bytes=60 << 20),
        name="traces",
    )(level, taken, table_of(mz), spectra.reshape(blocks, groups, 2 * fi, BLOCK), given)
    return traces.reshape(nt, rows, width)


def solution(mesh):
    return jax.shard_map(
        partial(body, mesh.shape["shot"], mesh.shape["freq"]),
        mesh=mesh,
        in_specs=(
            P(None, "freq", ("grp", "shot"), "rcv"),
            P(None, "freq", ("grp", "shot"), "rcv"),
            P(None, "freq", ("grp", "shot"), None),
            P(None, ("grp", "freq")),
            P(("grp", "shot")),
            P("grp"),
            P("grp"),
            P("grp"),
        ),
        out_specs=P("freq", ("grp", "shot"), "rcv"),
        check_vma=False,
    )
```

profile of v0, /device:TPU:1, one launch (start us, length us, event | category | flops | bytes accessed | tf_op | source)
XLA Modules:
  0.0 292.8 jit_solution(15723665657515301010)
XLA Ops:
  1.3 1.3 copy.12.pos
  2.6 0.8 mul.92
  3.4 1.7 copy.11
  5.1 2.3 cosine_convert_fusion
  7.5 0.8 copy.14.table
  8.3 0.9 copy.13.table
  9.2 269.7 %update.1 = (bf16[8,4,8,128,256]{4,3,2,1,0:T(8,128)(2,1)}, bf16[3,2048,256]{2,1,0:T(8,128)(2,1)}) custom-call(bf16[2,512,2048]{2,1,0:T(8,128)(2,1)} %bitcast.14, bf16[2,512,2048]{2,1,0:T(8,128)(2,1)} %bitcast.15, bf16[2,512,16]{2,1,0:T(8,128)(2,1)} %bitcast.16, f32[2,64]{1,0:T(2,128)} %wav.1, s32[8,1]{1,0:T(8,128)} %copy.12.pos, f32[1]{0:T(128)S(6)} %copy.16.step, ...), custom_call_target="tpu_custom_call" | custom-call | tf_op jit(solution)/shard_map/update/pallas_call | solution.py:421
  278.8 14.0 %traces.1 = bf16[2048,2048]{1,0:T(8,128)(2,1)} custom-call(f32[1]{0:T(128)S(6)} %div.3.level, s32[1]{0:T(128)} %bitcast.taken, bf16[256,512]{1,0:T(8,128)(2,1)} %copy.14.table, bf16[8,32,128,256]{3,2,1,0:T(8,128)(2,1)} %bitcast.13, bf16[3,2048,256]{2,1,0:T(8,128)(2,1)} %get-tuple-element.8.given), custom_call_target="tpu_custom_call" | custom-call | tf_op jit(solution)/shard_map/traces/pallas_call | solution.py:463
  (3 shorter events, 0.1 us)
where the time goes:
time: 293 us
  Pallas kernels  284 us (97%)
  local copies, waits for them, and re-layouts  5.5 us (2%)
    pallas_call x1, Pallas kernels, body(): pl.pallas_call(partial(update_kernel, nx, nz, nchunk, rows, lines, norm,...  270 us
    pallas_call x1, Pallas kernels, body(): pl.pallas_call(partial(trace_kernel, rows, t_group, gain, helped), out_sh...  14 us

commit v1 on v0

--- a/solution.py
+++ b/solution.py
@@ -481,9 +481,401 @@
     return traces.reshape(nt, rows, width)
 
 
+def relay_kernel(
+    nx, nz, nchunk, rows, lines, shots, norm, blocks, plain, early, gain, t_group,
+    data, est, win, wav, pos, bins, thr, step, out,
+    dbuf, ebuf, down, est_p, spec, mod_mine, mod_other, tables, sparse, made, obuf,
+    d_sem, e_sem, x_send, x_recv, c_send, c_recv, z_send, z_recv, o_sem,
+):
+    mx = lax.axis_index("shot")
+    mz = lax.axis_index("freq")
+    mc = lax.axis_index("rcv")
+    width = data.shape[2]
+    fl = FC * lines
+    fi = FC * rows
+    n = 2 * fi
+    part = nchunk * n
+    end = jnp.where(mz < 2, 0, 3)
+    inner = jnp.where(mz < 2, 1, 2)
+    is_end = mz == end
+    is_inner = jnp.logical_not(is_end)
+    level = thr[0].astype(jnp.float32) / 64.0
+
+    def load(ref, buf, sem, k):
+        return pltpu.make_async_copy(
+            ref.at[:, pl.ds(pl.multiple_of(k * fl, fl), fl)], buf.at[k], sem.at[k]
+        )
+
+    def load_all(k, carry):
+        load(data, dbuf, d_sem, k).start()
+        load(est, ebuf, e_sem, k).start()
+        return carry
+
+    lax.fori_loop(0, nchunk, load_all, 0)
+
+    barrier = pltpu.get_barrier_semaphore()
+    for d in range(1, nx):
+        pl.semaphore_signal(
+            barrier, inc=1, device_id={"shot": lax.rem(mx + d, nx)}, device_id_type=MESH
+        )
+    pl.semaphore_signal(barrier, inc=1, device_id={"rcv": 1 - mc}, device_id_type=MESH)
+    pl.semaphore_signal(
+        barrier, inc=1, device_id={"freq": jnp.where(is_end, inner, end)}, device_id_type=MESH
+    )
+
+    @pl.when(is_inner)
+    def _():
+        pl.semaphore_signal(barrier, inc=1, device_id={"freq": 3 - mz}, device_id_type=MESH)
+
+    pl.semaphore_wait(barrier, nx + 1 + is_inner.astype(jnp.int32))
+
+    def x_copy(d, k, piece):
+        here = down.at[k, :, pl.ds(piece * fl, fl)]
+        return pltpu.make_async_remote_copy(
+            src_ref=here, dst_ref=here,
+            send_sem=x_send.at[d, k], recv_sem=x_recv.at[d, k],
+            device_id={"shot": lax.rem(mx + d, nx)}, device_id_type=MESH,
+        )
+
+    def c_copy(k):
+        return pltpu.make_async_remote_copy(
+            src_ref=mod_mine.at[k], dst_ref=mod_other.at[k],
+            send_sem=c_send.at[k], recv_sem=c_recv.at[k],
+            device_id={"rcv": 1 - mc}, device_id_type=MESH,
+        )
+
+    def z_copy(kind, at, here, there, to):
+        return pltpu.make_async_remote_copy(
+            src_ref=here, dst_ref=there,
+            send_sem=z_send.at[kind, at], recv_sem=z_recv.at[kind, at],
+            device_id={"freq": to}, device_id_type=MESH,
+        )
+
+    def chunk_copy(kind, slot, k, lo, count, to):
+        row = pl.multiple_of(slot * part + k * n, n)
+        here = spec.at[pl.ds(lo, count), pl.ds(row, n)]
+        return z_copy(kind, k, here, here, to)
+
+    def block_copy(kind, slot, b, to):
+        here = spec.at[b, pl.ds(pl.multiple_of(slot * part, part), part)]
+        return z_copy(kind, b, here, here, to)
+
+    late = blocks - early
+    to_inner_early = lambda k: chunk_copy(0, end, k, 0, early, inner)
+    to_inner_late = lambda k: chunk_copy(1, end, k, early, late, inner)
+    across_own = lambda k, own: chunk_copy(2, own, k, 0, early, 3 - mz)
+    across_end = lambda k, of: chunk_copy(3, of, k, 0, early, 3 - mz)
+    out_own = lambda k: chunk_copy(4, inner, k, 0, plain, end)
+    out_opp = lambda k: chunk_copy(5, 3 - inner, k, 0, plain, end)
+    out_far = lambda k: chunk_copy(6, 3 - end, k, 0, plain, end)
+    block_own = lambda b, own: block_copy(7, own, b, 3 - mz)
+    block_end = lambda b, of: block_copy(8, of, b, 3 - mz)
+    landing = lambda b: spec.at[b, pl.ds(part, 2 * part)]
+    trace_copy = lambda b: z_copy(9, b, made.at[b - plain], landing(b), end)
+
+    def out_copy(src, b, sem):
+        return pltpu.make_async_copy(
+            src, out.at[:, pl.ds(pl.multiple_of(b * BLOCK, BLOCK), BLOCK)], sem
+        )
+
+    line, column = iota((lines, width), 0), mc * width + iota((lines, width), 1)
+    select = jnp.zeros((lines, width), jnp.float32)
+    for s in range(lines):
+        select = jnp.where((line == s) & (column == pos[s]), 1.0, select)
+
+    def make_down(k):
+        load(data, dbuf, d_sem, k).wait()
+        for c in range(2):
+            parts = []
+            lines_k = dbuf[k, c].astype(jnp.float32)
+            for f in range(FC):
+                w = wav[c, k * FC + f]
+                parts.append(w * select - lines_k[f * lines:(f + 1) * lines])
+            down[k, c, pl.ds(pl.multiple_of(mx * fl, fl), fl)] = jnp.concatenate(
+                parts, axis=0
+            ).astype(jnp.bfloat16)
+        for d in range(1, nx):
+            x_copy(d, k, mx).start()
+
+    dst, src = iota((n, n), 0), iota((n, n), 1)
+    want = (dst // FC % 2) * fi + (dst % FC) * rows + dst // (2 * FC)
+    perm = (src == want).astype(jnp.bfloat16)
+
+    def permute(k):
+        load(est, ebuf, e_sem, k).wait()
+        est_p[k] = jnp.dot(
+            perm, ebuf[k].reshape(n, width), preferred_element_type=jnp.float32
+        ).astype(jnp.bfloat16)
+
+    cols = nx * fl
+    nf = nchunk * FC
+    col3 = iota((2 * rows, shots, cols), 2)
+    shot_of = col3 // fl * lines + col3 % lines
+    own_shot = iota((2 * rows, shots, cols), 1) == shot_of
+    f_row, f_col = iota((nf, cols), 0), iota((nf, cols), 1) % fl // lines
+    shape3 = (rows, FC, cols)
+    same = iota(shape3, 1) == iota(shape3, 2) % fl // lines
+    scale = step[0]
+
+    def make_tables():
+        size = nz * nf
+        row, col = iota((size, 2 * size), 0), iota((size, 2 * size), 1)
+        match = row == col // (2 * FC) * FC + col % FC
+        to_re = (match & (col // FC % 2 == 0)).astype(jnp.bfloat16)
+        to_im = (match & (col // FC % 2 == 1)).astype(jnp.bfloat16)
+        nt = tables.shape[1]
+        for j, z in enumerate((mz, end)):
+            times = z * nt + iota((nt, size), 0)
+            phase = times * bins[...] % NT
+            angle = 2.0 * math.pi / NT * phase.astype(jnp.float32)
+            tables[j] = (
+                jnp.dot(jnp.cos(angle).astype(jnp.bfloat16), to_re,
+                        preferred_element_type=jnp.float32)
+                + jnp.dot((-jnp.sin(angle)).astype(jnp.bfloat16), to_im,
+                          preferred_element_type=jnp.float32)
+            ).astype(jnp.bfloat16)
+
+    def model(k):
+        for d in range(1, nx):
+            x_copy(d, k, lax.rem(mx + nx - d, nx)).wait_recv()
+        lines_k = down[k].reshape(2 * cols, width)
+        m = lax.dot_general(
+            est_p[k], lines_k, (((1,), (1,)), ((), ())), preferred_element_type=jnp.float32
+        ).reshape(rows, 2, FC, 2 * cols)
+        mod_mine[k, 0] = m[:, 0, :, :cols] - m[:, 1, :, cols:]
+        mod_mine[k, 1] = m[:, 0, :, cols:] + m[:, 1, :, :cols]
+        c_copy(k).start()
+
+    def update(k):
+        pick = (f_row == k * FC + f_col).astype(jnp.bfloat16)
+        w = jnp.dot(win[...], pick, preferred_element_type=jnp.float32)
+        w = jnp.where(own_shot, w.reshape(2 * rows, shots, cols), 0.0).sum(axis=1)
+        c_copy(k).wait_recv()
+        total_re = mod_mine[k, 0] + mod_other[k, 0]
+        total_im = mod_mine[k, 1] + mod_other[k, 1]
+        e_re = jnp.where(same, w[:rows, None, :] - total_re, 0.0)
+        e_im = jnp.where(same, w[rows:, None, :] - total_im, 0.0)
+        e = jnp.stack(
+            [jnp.concatenate([e_re, e_im], axis=2), jnp.concatenate([e_im, -e_re], axis=2)], axis=1
+        ).reshape(n, 2 * cols).astype(jnp.bfloat16)
+        grad = jnp.dot(e, down[k].reshape(2 * cols, width), preferred_element_type=jnp.float32)
+        new = (est_p[k].astype(jnp.float32) - scale * (grad * norm)).astype(jnp.bfloat16)
+        row = pl.multiple_of(mz * part + k * n, n)
+        for b in range(blocks):
+            spec[b, pl.ds(row, n)] = new[:, b * BLOCK:(b + 1) * BLOCK]
+
+    def send(k):
+        @pl.when(is_end)
+        def _():
+            to_inner_early(k).start()
+            to_inner_late(k).start()
+
+        @pl.when(is_inner)
+        def _():
+            across_own(k, mz).start()
+            out_own(k).start()
+
+    def relay(k):
+        @pl.when(is_inner & (k >= 1) & (k <= nchunk))
+        def _():
+            to_inner_early(k - 1).wait_recv()
+            across_end(k - 1, end).start()
+            across_own(k - 1, 3 - mz).wait_recv()
+            out_opp(k - 1).start()
+
+        @pl.when(is_inner & (k >= 2))
+        def _():
+            across_end(k - 2, 3 - end).wait_recv()
+            out_far(k - 2).start()
+
+    make_down(0)
+    make_down(1)
+    permute(0)
+
+    def step_of(k, carry):
+        @pl.when(k < nchunk - 2)
+        def _():
+            make_down(k + 2)
+
+        @pl.when(k < nchunk - 1)
+        def _():
+            permute(k + 1)
+
+        @pl.when(k == 2)
+        def _():
+            make_tables()
+
+        @pl.when(k < nchunk)
+        def _():
+            model(k)
+            update(k)
+            send(k)
+
+        relay(k)
+        return carry
+
+    lax.fori_loop(0, nchunk + 2, step_of, 0)
+
+    def traces(b, table, to):
+        make_traces(
+            spec.at[b].reshape(nz * nchunk, n, BLOCK), table, level, gain, rows, t_group,
+            sparse, to,
+        )
+
+    def own_block(b):
+        at = lax.rem(b, 2)
+
+        @pl.when(b >= 2)
+        def _():
+            out_copy(obuf.at[at], b - 2, o_sem.at[b - 2]).wait()
+
+        traces(b, tables.at[0], obuf.at[at])
+        out_copy(obuf.at[at], b, o_sem.at[b]).start()
+
+    def help_block(b):
+        traces(b, tables.at[1], made.at[b - plain])
+        trace_copy(b).start()
+
+    def loop(lo, hi, f):
+        def one(i, carry):
+            f(i)
+            return carry
+
+        lax.fori_loop(lo, hi, one, 0)
+
+    @pl.when(is_inner)
+    def _():
+        loop(0, nchunk, lambda k: to_inner_late(k).wait_recv())
+
+        def hand_on(b):
+            block_own(b, mz).start()
+            block_end(b, end).start()
+
+        loop(early, blocks, hand_on)
+
+        loop(plain, early, help_block)
+        loop(0, early, own_block)
+
+        def rest(b):
+            block_own(b, 3 - mz).wait_recv()
+            block_end(b, 3 - end).wait_recv()
+            help_block(b)
+            own_block(b)
+
+        loop(early, blocks, rest)
+        loop(blocks - 2, blocks, lambda b: out_copy(obuf.at[lax.rem(b, 2)], b, o_sem.at[b]).wait())
+
+        def drain(k):
+            across_own(k, mz).wait_send()
+            across_end(k, end).wait_send()
+            out_own(k).wait_send()
+            out_opp(k).wait_send()
+            out_far(k).wait_send()
+
+        loop(0, nchunk, drain)
+
+        def drain_block(b):
+            block_own(b, mz).wait_send()
+            block_end(b, end).wait_send()
+
+        loop(early, blocks, drain_block)
+        loop(plain, blocks, lambda b: trace_copy(b).wait_send())
+
+    @pl.when(is_end)
+    def _():
+        def arrived(k):
+            out_own(k).wait_recv()
+            out_opp(k).wait_recv()
+            out_far(k).wait_recv()
+
+        loop(0, nchunk, arrived)
+        loop(0, plain, own_block)
+        loop(plain - 2, plain, lambda b: out_copy(obuf.at[lax.rem(b, 2)], b, o_sem.at[b]).wait())
+
+        def take(b):
+            trace_copy(b).wait_recv()
+            out_copy(landing(b), b, o_sem.at[b]).start()
+
+        loop(plain, blocks, take)
+        loop(plain, blocks, lambda b: out_copy(landing(b), b, o_sem.at[b]).wait())
+
+        def drain(k):
+            to_inner_early(k).wait_send()
+            to_inner_late(k).wait_send()
+
+        loop(0, nchunk, drain)
+
+    def drain(k):
+        for d in range(1, nx):
+            x_copy(d, k, mx).wait_send()
+        c_copy(k).wait_send()
+
+    loop(0, nchunk, drain)
+
+
+def relay_body(nx, nz, data, estimate, window_data, wavelet, positions, bins, threshold, step):
+    _, nf, lines, width = data.shape
+    rows = estimate.shape[2]
+    shots = window_data.shape[3]
+    nchunk = nf // FC
+    norm = 1.0 / math.sqrt(shots * RCV)
+    fi, cols = FC * rows, nx * FC * lines
+    nt = NT // nz
+    blocks = width // BLOCK
+    plain, early = 3 * blocks // 8, blocks // 2
+    gain, t_group = math.sqrt(RCV / NF), 32
+
+    vmem = pl.BlockSpec(memory_space=pltpu.VMEM)
+    smem = pl.BlockSpec(memory_space=pltpu.SMEM)
+    hbm = pl.BlockSpec(memory_space=pl.ANY)
+    dma = pltpu.SemaphoreType.DMA
+    traces = pl.pallas_call(
+        partial(
+            relay_kernel, nx, nz, nchunk, rows, lines, shots, norm, blocks, plain, early,
+            gain, t_group,
+        ),
+        out_shape=jax.ShapeDtypeStruct((nt * rows, width), jnp.bfloat16),
+        in_specs=[hbm, hbm, vmem, smem, smem, vmem, smem, smem],
+        out_specs=hbm,
+        scratch_shapes=[
+            pltpu.VMEM((nchunk, 2, FC * lines, width), jnp.bfloat16),
+            pltpu.VMEM((nchunk, 2, FC * rows, width), jnp.bfloat16),
+            pltpu.VMEM((nchunk, 2, cols, width), jnp.bfloat16),
+            pltpu.VMEM((nchunk, 2 * fi, width), jnp.bfloat16),
+            pltpu.VMEM((blocks, nz * nchunk * 2 * fi, BLOCK), jnp.bfloat16),
+            pltpu.VMEM((nchunk, 2, rows, FC, cols), jnp.float32),
+            pltpu.VMEM((nchunk, 2, rows, FC, cols), jnp.float32),
+            pltpu.VMEM((2, nt, 2 * nz * nf), jnp.bfloat16),
+            pltpu.VMEM((rows, nt, BLOCK), jnp.bfloat16),
+            pltpu.VMEM((blocks - plain, nt * rows, BLOCK), jnp.bfloat16),
+            pltpu.VMEM((2, nt * rows, BLOCK), jnp.bfloat16),
+            dma((nchunk,)), dma((nchunk,)),
+            dma((nx, nchunk)), dma((nx, nchunk)),
+            dma((nchunk,)), dma((nchunk,)),
+            dma((10, max(nchunk, blocks))), dma((10, max(nchunk, blocks))),
+            dma((blocks,)),
+        ],
+        compiler_params=pltpu.CompilerParams(
+            collective_id=1, has_side_effects=True, vmem_limit_bytes=60 << 20
+        ),
+        name="relay",
+    )(
+        data.reshape(2, nf * lines, width),
+        estimate.reshape(2, nf * rows, width),
+        window_data.transpose(0, 2, 3, 1).reshape(2 * rows * shots, nf),
+        wavelet,
+        positions,
+        bins.reshape(1, nz * nf),
+        threshold,
+        step,
+    )
+    return traces.reshape(nt, rows, width)
+
+
 def solution(mesh):
+    nz = mesh.shape["freq"]
     return jax.shard_map(
-        partial(body, mesh.shape["shot"], mesh.shape["freq"]),
+        partial(relay_body if nz == 4 else body, mesh.shape["shot"], nz),
         mesh=mesh,
         in_specs=(
             P(None, "freq", ("grp", "shot"), "rcv"),

time: 293 us -> 259 us (0.88)
  Pallas kernels: 284 us -> 249 us
  local copies, waits for them, and re-layouts: 5.5 us -> 8.44 us
    pallas_call x2 -> x1, Pallas kernels: 284 us -> 249 us  [relay_body(): pl.pallas_call(partial(relay_kernel, nx, nz, nchunk, rows, lines, shots,...]
    unnamed x1, local copies, waits for them, and re-layouts: 1.72 us -> 8.44 us
where the time goes in v1:
time: 259 us; the launch traced here: 258 us
  Pallas kernels  249 us (96%)
  local copies, waits for them, and re-layouts  8.44 us (3%)
    pallas_call x1, Pallas kernels, relay_body(): pl.pallas_call(partial(relay_kernel, nx, nz, nchunk, rows, lines, shots,...  249 us
    unnamed x1, local copies, waits for them, and re-layouts  8.44 us

profile of v1, /device:TPU:1, one launch (start us, length us, event | category | flops | bytes accessed | tf_op | source)
XLA Modules:
  0.0 258.4 jit_solution(1334576000207498503)
XLA Ops:
  1.3 248.7 %relay.1 = bf16[2048,2048]{1,0:T(8,128)(2,1)} custom-call(bf16[2,512,2048]{2,1,0:T(8,128)(2,1)} %bitcast.8, bf16[2,512,2048]{2,1,0:T(8,128)(2,1)} %bitcast.9, bf16[256,64]{1,0:T(8,128)(2,1)} %bitcast.10, f32[2,64]{1,0:T(2,128)} %wav.1, s32[8]{0:T(128)} %pos.1, s32[1,256]{1,0:T(1,128)} %bitcast.11, s32[1]{0:T(128)S(6)} %copy.10.thr, f32[1]{0:T(128)S(6)} %copy.11.step), custom_call_target="tpu_custom_call" | custom-call | tf_op jit(solution)/shard_map/relay/pallas_call | solution.py:832
  250.0 8.4 %copy.12 = bf16[256,8,2048]{2,1,0:T(8,128)(2,1)} copy(bf16[256,8,2048]{2,1,0:T(8,128)(2,1)} %bitcast.7) | data formatting | bytes 16777216

commit v2 on v1

--- a/solution.py
+++ b/solution.py
@@ -12,6 +12,8 @@
 RCV = 4096
 NT = 1024
 FC = 8
+GF = 4
+PAIR = 2
 BLOCK = 256
 LAG = 1
 MESH = pl.DeviceIdType.MESH
@@ -481,18 +483,37 @@
     return traces.reshape(nt, rows, width)
 
 
+def make_pairs(u, table, lv, gain, rows, t_group, sparse, out):
+    groups, _, width = u.shape
+    part = 2 * GF * PAIR
+    nt = table.shape[0] // PAIR
+    for p in range(rows // PAIR):
+        up = u[:, p * part:(p + 1) * part, :].reshape(groups * part, width)
+        tr = jnp.dot(table[...], up, preferred_element_type=jnp.float32) * gain
+        sparse[p] = (jnp.maximum(tr - lv, 0.0) + jnp.minimum(tr + lv, 0.0)).astype(jnp.bfloat16)
+    lined = sparse.reshape(rows, nt, width)
+    n = t_group * rows
+    dst, src = iota((n, n), 0), iota((n, n), 1)
+    perm = (src == (dst % rows) * t_group + dst // rows).astype(jnp.bfloat16)
+    for g in range(nt // t_group):
+        x = lined[:, g * t_group:(g + 1) * t_group, :].reshape(n, width)
+        out[g * n:(g + 1) * n, :] = jnp.dot(
+            perm, x, preferred_element_type=jnp.float32
+        ).astype(jnp.bfloat16)
+
+
 def relay_kernel(
     nx, nz, nchunk, rows, lines, shots, norm, blocks, plain, early, gain, t_group,
     data, est, win, wav, pos, bins, thr, step, out,
-    dbuf, ebuf, down, est_p, spec, mod_mine, mod_other, tables, sparse, made, obuf,
-    d_sem, e_sem, x_send, x_recv, c_send, c_recv, z_send, z_recv, o_sem,
+    dbuf, ebuf, down, spec, mod_mine, mod_other, tables, sparse, made,
+    d_sem, e_sem, x_send, x_recv, c_send, c_recv, z_send, z_recv,
 ):
     mx = lax.axis_index("shot")
     mz = lax.axis_index("freq")
     mc = lax.axis_index("rcv")
     width = data.shape[2]
-    fl = FC * lines
-    fi = FC * rows
+    fl = GF * lines
+    fi = GF * rows
     n = 2 * fi
     part = nchunk * n
     end = jnp.where(mz < 2, 0, 3)
@@ -570,13 +591,7 @@
     out_far = lambda k: chunk_copy(6, 3 - end, k, 0, plain, end)
     block_own = lambda b, own: block_copy(7, own, b, 3 - mz)
     block_end = lambda b, of: block_copy(8, of, b, 3 - mz)
-    landing = lambda b: spec.at[b, pl.ds(part, 2 * part)]
-    trace_copy = lambda b: z_copy(9, b, made.at[b - plain], landing(b), end)
-
-    def out_copy(src, b, sem):
-        return pltpu.make_async_copy(
-            src, out.at[:, pl.ds(pl.multiple_of(b * BLOCK, BLOCK), BLOCK)], sem
-        )
+    trace_copy = lambda b: z_copy(9, b, made.at[b - plain], out.at[b], end)
 
     line, column = iota((lines, width), 0), mc * width + iota((lines, width), 1)
     select = jnp.zeros((lines, width), jnp.float32)
@@ -588,8 +603,8 @@
         for c in range(2):
             parts = []
             lines_k = dbuf[k, c].astype(jnp.float32)
-            for f in range(FC):
-                w = wav[c, k * FC + f]
+            for f in range(GF):
+                w = wav[c, k * GF + f]
                 parts.append(w * select - lines_k[f * lines:(f + 1) * lines])
             down[k, c, pl.ds(pl.multiple_of(mx * fl, fl), fl)] = jnp.concatenate(
                 parts, axis=0
@@ -598,68 +613,73 @@
             x_copy(d, k, mx).start()
 
     dst, src = iota((n, n), 0), iota((n, n), 1)
-    want = (dst // FC % 2) * fi + (dst % FC) * rows + dst // (2 * FC)
+    want = (dst // GF % 2) * fi + (dst % GF) * rows + dst // (2 * GF)
     perm = (src == want).astype(jnp.bfloat16)
 
-    def permute(k):
-        load(est, ebuf, e_sem, k).wait()
-        est_p[k] = jnp.dot(
-            perm, ebuf[k].reshape(n, width), preferred_element_type=jnp.float32
-        ).astype(jnp.bfloat16)
-
     cols = nx * fl
-    nf = nchunk * FC
+    nf = nchunk * GF
     col3 = iota((2 * rows, shots, cols), 2)
     shot_of = col3 // fl * lines + col3 % lines
     own_shot = iota((2 * rows, shots, cols), 1) == shot_of
     f_row, f_col = iota((nf, cols), 0), iota((nf, cols), 1) % fl // lines
-    shape3 = (rows, FC, cols)
-    same = iota(shape3, 1) == iota(shape3, 2) % fl // lines
+    shape3 = (GF, rows, cols)
+    same = iota(shape3, 0) == iota(shape3, 2) % fl // lines
     scale = step[0]
 
-    def make_tables():
-        size = nz * nf
-        row, col = iota((size, 2 * size), 0), iota((size, 2 * size), 1)
-        match = row == col // (2 * FC) * FC + col % FC
-        to_re = (match & (col // FC % 2 == 0)).astype(jnp.bfloat16)
-        to_im = (match & (col // FC % 2 == 1)).astype(jnp.bfloat16)
-        nt = tables.shape[1]
-        for j, z in enumerate((mz, end)):
-            times = z * nt + iota((nt, size), 0)
-            phase = times * bins[...] % NT
-            angle = 2.0 * math.pi / NT * phase.astype(jnp.float32)
-            tables[j] = (
-                jnp.dot(jnp.cos(angle).astype(jnp.bfloat16), to_re,
-                        preferred_element_type=jnp.float32)
-                + jnp.dot((-jnp.sin(angle)).astype(jnp.bfloat16), to_im,
-                          preferred_element_type=jnp.float32)
-            ).astype(jnp.bfloat16)
+    def make_table(j, z):
+        size, nt = nz * nf, sparse.shape[1] // PAIR
+        wide = 2 * PAIR * size
+        row, col = iota((size, wide), 0), iota((size, wide), 1)
+        match = row == col // (2 * GF * PAIR) * GF + col % GF
+        to_re = (match & (col // GF % 2 == 0)).astype(jnp.bfloat16)
+        to_im = (match & (col // GF % 2 == 1)).astype(jnp.bfloat16)
+        times = z * nt + iota((nt, size), 0)
+        phase = times * bins[...] % NT
+        angle = 2.0 * math.pi / NT * phase.astype(jnp.float32)
+        full = jnp.dot(
+            jnp.cos(angle).astype(jnp.bfloat16), to_re, preferred_element_type=jnp.float32
+        ) + jnp.dot(
+            (-jnp.sin(angle)).astype(jnp.bfloat16), to_im, preferred_element_type=jnp.float32
+        )
+        member = iota((nt, wide), 1) // (2 * GF) % PAIR
+        for a in range(PAIR):
+            tables[j, a * nt:(a + 1) * nt] = jnp.where(member == a, full, 0.0).astype(
+                jnp.bfloat16
+            )
+
+    def spectra_of(k):
+        return ebuf[k].reshape(n, width)
 
     def model(k):
+        load(est, ebuf, e_sem, k).wait()
         for d in range(1, nx):
             x_copy(d, k, lax.rem(mx + nx - d, nx)).wait_recv()
-        lines_k = down[k].reshape(2 * cols, width)
-        m = lax.dot_general(
-            est_p[k], lines_k, (((1,), (1,)), ((), ())), preferred_element_type=jnp.float32
-        ).reshape(rows, 2, FC, 2 * cols)
-        mod_mine[k, 0] = m[:, 0, :, :cols] - m[:, 1, :, cols:]
-        mod_mine[k, 1] = m[:, 0, :, cols:] + m[:, 1, :, :cols]
+        m_re, m_im = [
+            lax.dot_general(
+                spectra_of(k), down[k, c], (((1,), (1,)), ((), ())),
+                preferred_element_type=jnp.float32,
+            )
+            for c in range(2)
+        ]
+        mod_mine[k, 0] = m_re[:fi] - m_im[fi:]
+        mod_mine[k, 1] = m_im[:fi] + m_re[fi:]
         c_copy(k).start()
 
     def update(k):
-        pick = (f_row == k * FC + f_col).astype(jnp.bfloat16)
+        pick = (f_row == k * GF + f_col).astype(jnp.bfloat16)
         w = jnp.dot(win[...], pick, preferred_element_type=jnp.float32)
         w = jnp.where(own_shot, w.reshape(2 * rows, shots, cols), 0.0).sum(axis=1)
         c_copy(k).wait_recv()
-        total_re = mod_mine[k, 0] + mod_other[k, 0]
-        total_im = mod_mine[k, 1] + mod_other[k, 1]
-        e_re = jnp.where(same, w[:rows, None, :] - total_re, 0.0)
-        e_im = jnp.where(same, w[rows:, None, :] - total_im, 0.0)
-        e = jnp.stack(
-            [jnp.concatenate([e_re, e_im], axis=2), jnp.concatenate([e_im, -e_re], axis=2)], axis=1
-        ).reshape(n, 2 * cols).astype(jnp.bfloat16)
+        total_re = (mod_mine[k, 0] + mod_other[k, 0]).reshape(shape3)
+        total_im = (mod_mine[k, 1] + mod_other[k, 1]).reshape(shape3)
+        e_re = jnp.where(same, w[None, :rows] - total_re, 0.0).reshape(fi, cols)
+        e_im = jnp.where(same, w[None, rows:] - total_im, 0.0).reshape(fi, cols)
+        e = jnp.concatenate(
+            [jnp.concatenate([e_re, e_im], axis=1), jnp.concatenate([e_im, -e_re], axis=1)], axis=0
+        ).astype(jnp.bfloat16)
         grad = jnp.dot(e, down[k].reshape(2 * cols, width), preferred_element_type=jnp.float32)
-        new = (est_p[k].astype(jnp.float32) - scale * (grad * norm)).astype(jnp.bfloat16)
+        new = (spectra_of(k).astype(jnp.float32) - scale * (grad * norm)).astype(jnp.bfloat16)
+        new = jnp.dot(perm, new, preferred_element_type=jnp.float32).astype(jnp.bfloat16)
         row = pl.multiple_of(mz * part + k * n, n)
         for b in range(blocks):
             spec[b, pl.ds(row, n)] = new[:, b * BLOCK:(b + 1) * BLOCK]
@@ -690,20 +710,16 @@
 
     make_down(0)
     make_down(1)
-    permute(0)
 
     def step_of(k, carry):
         @pl.when(k < nchunk - 2)
         def _():
             make_down(k + 2)
 
-        @pl.when(k < nchunk - 1)
-        def _():
-            permute(k + 1)
-
-        @pl.when(k == 2)
-        def _():
-            make_tables()
+        for j, z in enumerate((mz, end)):
+            @pl.when(k == nchunk // 4 * (j + 1))
+            def _():
+                make_table(j, z)
 
         @pl.when(k < nchunk)
         def _():
@@ -717,20 +733,13 @@
     lax.fori_loop(0, nchunk + 2, step_of, 0)
 
     def traces(b, table, to):
-        make_traces(
+        make_pairs(
             spec.at[b].reshape(nz * nchunk, n, BLOCK), table, level, gain, rows, t_group,
             sparse, to,
         )
 
     def own_block(b):
-        at = lax.rem(b, 2)
-
-        @pl.when(b >= 2)
-        def _():
-            out_copy(obuf.at[at], b - 2, o_sem.at[b - 2]).wait()
-
-        traces(b, tables.at[0], obuf.at[at])
-        out_copy(obuf.at[at], b, o_sem.at[b]).start()
+        traces(b, tables.at[0], out.at[b])
 
     def help_block(b):
         traces(b, tables.at[1], made.at[b - plain])
@@ -763,7 +772,6 @@
             own_block(b)
 
         loop(early, blocks, rest)
-        loop(blocks - 2, blocks, lambda b: out_copy(obuf.at[lax.rem(b, 2)], b, o_sem.at[b]).wait())
 
         def drain(k):
             across_own(k, mz).wait_send()
@@ -790,14 +798,7 @@
 
         loop(0, nchunk, arrived)
         loop(0, plain, own_block)
-        loop(plain - 2, plain, lambda b: out_copy(obuf.at[lax.rem(b, 2)], b, o_sem.at[b]).wait())
-
-        def take(b):
-            trace_copy(b).wait_recv()
-            out_copy(landing(b), b, o_sem.at[b]).start()
-
-        loop(plain, blocks, take)
-        loop(plain, blocks, lambda b: out_copy(landing(b), b, o_sem.at[b]).wait())
+        loop(plain, blocks, lambda b: trace_copy(b).wait_recv())
 
         def drain(k):
             to_inner_early(k).wait_send()
@@ -813,13 +814,27 @@
     loop(0, nchunk, drain)
 
 
+def place_kernel(traces, out, sem):
+    copies = [
+        pltpu.make_async_copy(
+            traces.at[b], out.at[:, pl.ds(b * BLOCK, BLOCK)], sem.at[b]
+        )
+        for b in range(traces.shape[0])
+    ]
+    for copy in copies:
+        copy.start()
+    for copy in copies:
+        copy.wait()
+
+
 def relay_body(nx, nz, data, estimate, window_data, wavelet, positions, bins, threshold, step):
     _, nf, lines, width = data.shape
     rows = estimate.shape[2]
     shots = window_data.shape[3]
-    nchunk = nf // FC
+    nchunk = nf // GF
     norm = 1.0 / math.sqrt(shots * RCV)
-    fi, cols = FC * rows, nx * FC * lines
+    fi, cols = GF * rows, nx * GF * lines
+    size = nz * nf
     nt = NT // nz
     blocks = width // BLOCK
     plain, early = 3 * blocks // 8, blocks // 2
@@ -834,29 +849,26 @@
             relay_kernel, nx, nz, nchunk, rows, lines, shots, norm, blocks, plain, early,
             gain, t_group,
         ),
-        out_shape=jax.ShapeDtypeStruct((nt * rows, width), jnp.bfloat16),
+        out_shape=pltpu.VMEM((blocks, nt * rows, BLOCK), jnp.bfloat16),
         in_specs=[hbm, hbm, vmem, smem, smem, vmem, smem, smem],
-        out_specs=hbm,
+        out_specs=vmem,
         scratch_shapes=[
-            pltpu.VMEM((nchunk, 2, FC * lines, width), jnp.bfloat16),
-            pltpu.VMEM((nchunk, 2, FC * rows, width), jnp.bfloat16),
+            pltpu.VMEM((nchunk, 2, GF * lines, width), jnp.bfloat16),
+            pltpu.VMEM((nchunk, 2, fi, width), jnp.bfloat16),
             pltpu.VMEM((nchunk, 2, cols, width), jnp.bfloat16),
-            pltpu.VMEM((nchunk, 2 * fi, width), jnp.bfloat16),
             pltpu.VMEM((blocks, nz * nchunk * 2 * fi, BLOCK), jnp.bfloat16),
-            pltpu.VMEM((nchunk, 2, rows, FC, cols), jnp.float32),
-            pltpu.VMEM((nchunk, 2, rows, FC, cols), jnp.float32),
-            pltpu.VMEM((2, nt, 2 * nz * nf), jnp.bfloat16),
-            pltpu.VMEM((rows, nt, BLOCK), jnp.bfloat16),
+            pltpu.VMEM((nchunk, 2, fi, cols), jnp.float32),
+            pltpu.VMEM((nchunk, 2, fi, cols), jnp.float32),
+            pltpu.VMEM((2, PAIR * nt, 2 * PAIR * size), jnp.bfloat16),
+            pltpu.VMEM((rows // PAIR, PAIR * nt, BLOCK), jnp.bfloat16),
             pltpu.VMEM((blocks - plain, nt * rows, BLOCK), jnp.bfloat16),
-            pltpu.VMEM((2, nt * rows, BLOCK), jnp.bfloat16),
             dma((nchunk,)), dma((nchunk,)),
             dma((nx, nchunk)), dma((nx, nchunk)),
             dma((nchunk,)), dma((nchunk,)),
             dma((10, max(nchunk, blocks))), dma((10, max(nchunk, blocks))),
-            dma((blocks,)),
         ],
         compiler_params=pltpu.CompilerParams(
-            collective_id=1, has_side_effects=True, vmem_limit_bytes=60 << 20
+            collective_id=1, has_side_effects=True, vmem_limit_bytes=48 << 20
         ),
         name="relay",
     )(
@@ -865,11 +877,20 @@
         window_data.transpose(0, 2, 3, 1).reshape(2 * rows * shots, nf),
         wavelet,
         positions,
-        bins.reshape(1, nz * nf),
+        bins.reshape(1, size),
         threshold,
         step,
     )
-    return traces.reshape(nt, rows, width)
+    placed = pl.pallas_call(
+        place_kernel,
+        out_shape=jax.ShapeDtypeStruct((nt * rows, width), jnp.bfloat16),
+        in_specs=[vmem],
+        out_specs=hbm,
+        scratch_shapes=[dma((blocks,))],
+        compiler_params=pltpu.CompilerParams(vmem_limit_bytes=4 << 20),
+        name="place",
+    )(traces)
+    return placed.reshape(nt, rows, width)
 
 
 def solution(mesh):

time: 259 us -> 244 us (0.942)
  local copies, waits for them, and re-layouts: 8.44 us -> 0 us
  Pallas kernels: 249 us -> 242 us
    pallas_call x1, Pallas kernels: 249 us -> 239 us  [relay_body(): pl.pallas_call(partial(relay_kernel, nx, nz, nchunk, rows, lines, shots,...]
    unnamed x1 -> x0, local copies, waits for them, and re-layouts: 8.44 us -> none
    pallas_call x0 -> x1, Pallas kernels: none -> 3.37 us  [relay_body(): pl.pallas_call(place_kernel, out_shape=jax.ShapeDtypeStruct((nt * rows, w...]
where the time goes in v2:
time: 244 us
  Pallas kernels  242 us (99%)
    pallas_call x1, Pallas kernels, relay_body(): pl.pallas_call(partial(relay_kernel, nx, nz, nchunk, rows, lines, shots,...  239 us

profile of v2, /device:TPU:1, one launch (start us, length us, event | category | flops | bytes accessed | tf_op | source)
XLA Modules:
  0.0 243.8 jit_solution(12872524463046251992)
XLA Ops:
  1.3 239.1 %relay.1.traces = bf16[8,2048,256]{2,1,0:T(8,128)(2,1)S(1)} custom-call(bf16[2,512,2048]{2,1,0:T(8,128)(2,1)} %bitcast.7, bf16[2,512,2048]{2,1,0:T(8,128)(2,1)} %bitcast.8, bf16[256,64]{1,0:T(8,128)(2,1)} %bitcast.9, f32[2,64]{1,0:T(2,128)} %wav.1, s32[8]{0:T(128)} %pos.1, s32[1,256]{1,0:T(1,128)} %bitcast.10, s32[1]{0:T(128)S(6)} %copy.9.thr, f32[1]{0:T(128)S(6)} %copy.10.step), custom_call_target="tpu_custom_call" | custom-call | tf_op jit(solution)/shard_map/relay/pallas_call | solution.py:847
  240.4 3.4 %place.1 = bf16[2048,2048]{1,0:T(8,128)(2,1)} custom-call(bf16[8,2048,256]{2,1,0:T(8,128)(2,1)S(1)} %relay.1.traces), custom_call_target="tpu_custom_call" | custom-call | tf_op jit(solution)/shard_map/place/pallas_call | solution.py:884

commit v3 on v2

--- a/solution.py
+++ b/solution.py
@@ -14,6 +14,8 @@
 FC = 8
 GF = 4
 PAIR = 2
+TILE = 128
+PLAIN = 5
 BLOCK = 256
 LAG = 1
 MESH = pl.DeviceIdType.MESH
@@ -483,28 +485,35 @@
     return traces.reshape(nt, rows, width)
 
 
-def make_pairs(u, table, lv, gain, rows, t_group, sparse, out):
-    groups, _, width = u.shape
+def make_pairs(spec, b, table, lv, gain, rows, t_group, sparse, out, at):
+    groups = spec.shape[0]
     part = 2 * GF * PAIR
     nt = table.shape[0] // PAIR
     for p in range(rows // PAIR):
-        up = u[:, p * part:(p + 1) * part, :].reshape(groups * part, width)
+        up = jnp.concatenate(
+            [
+                spec[:, b + h, p * part:(p + 1) * part].reshape(groups * part, TILE)
+                for h in range(2)
+            ],
+            axis=1,
+        )
         tr = jnp.dot(table[...], up, preferred_element_type=jnp.float32) * gain
         sparse[p] = (jnp.maximum(tr - lv, 0.0) + jnp.minimum(tr + lv, 0.0)).astype(jnp.bfloat16)
-    lined = sparse.reshape(rows, nt, width)
+    lined = sparse.reshape(rows, nt, 2 * TILE)
     n = t_group * rows
     dst, src = iota((n, n), 0), iota((n, n), 1)
     perm = (src == (dst % rows) * t_group + dst // rows).astype(jnp.bfloat16)
     for g in range(nt // t_group):
-        x = lined[:, g * t_group:(g + 1) * t_group, :].reshape(n, width)
-        out[g * n:(g + 1) * n, :] = jnp.dot(
-            perm, x, preferred_element_type=jnp.float32
-        ).astype(jnp.bfloat16)
+        x = lined[:, g * t_group:(g + 1) * t_group, :].reshape(n, 2 * TILE)
+        y = jnp.dot(perm, x, preferred_element_type=jnp.float32).astype(jnp.bfloat16)
+        for h in range(2):
+            out[at + h, g * n:(g + 1) * n, :] = y[:, h * TILE:(h + 1) * TILE]
 
 
 def relay_kernel(
     nx, nz, nchunk, rows, lines, shots, norm, blocks, plain, early, gain, t_group,
-    data, est, win, wav, pos, bins, thr, step, out,
+    data, est, win_in, wav_in, pos_in, bins_in, thr_in, step_in, out,
+    win, wav, pos, bins, thr, step, i_sem,
     dbuf, ebuf, down, spec, mod_mine, mod_other, tables, sparse, made,
     d_sem, e_sem, x_send, x_recv, c_send, c_recv, z_send, z_recv,
 ):
@@ -515,24 +524,31 @@
     fl = GF * lines
     fi = GF * rows
     n = 2 * fi
-    part = nchunk * n
     end = jnp.where(mz < 2, 0, 3)
     inner = jnp.where(mz < 2, 1, 2)
     is_end = mz == end
+    wide = mc == 0
+    first = plain + wide.astype(jnp.int32)
     is_inner = jnp.logical_not(is_end)
-    level = thr[0].astype(jnp.float32) / 64.0
+
+    smalls = [
+        pltpu.make_async_copy(src, dst, i_sem.at[i])
+        for i, (src, dst) in enumerate(
+            ((pos_in, pos), (wav_in, wav), (win_in, win), (step_in, step), (thr_in, thr),
+             (bins_in, bins))
+        )
+    ]
 
     def load(ref, buf, sem, k):
         return pltpu.make_async_copy(
             ref.at[:, pl.ds(pl.multiple_of(k * fl, fl), fl)], buf.at[k], sem.at[k]
         )
 
-    def load_all(k, carry):
-        load(data, dbuf, d_sem, k).start()
-        load(est, ebuf, e_sem, k).start()
-        return carry
-
-    lax.fori_loop(0, nchunk, load_all, 0)
+    for copy in smalls[:2]:
+        copy.start()
+    load(data, dbuf, d_sem, 0).start()
+    for copy in smalls[2:]:
+        copy.start()
 
     barrier = pltpu.get_barrier_semaphore()
     for d in range(1, nx):
@@ -540,15 +556,12 @@
             barrier, inc=1, device_id={"shot": lax.rem(mx + d, nx)}, device_id_type=MESH
         )
     pl.semaphore_signal(barrier, inc=1, device_id={"rcv": 1 - mc}, device_id_type=MESH)
-    pl.semaphore_signal(
-        barrier, inc=1, device_id={"freq": jnp.where(is_end, inner, end)}, device_id_type=MESH
-    )
+    for z in (jnp.where(is_end, inner, end), jnp.where(is_end, 3 - inner, 3 - end)):
+        pl.semaphore_signal(barrier, inc=1, device_id={"freq": z}, device_id_type=MESH)
 
     @pl.when(is_inner)
     def _():
         pl.semaphore_signal(barrier, inc=1, device_id={"freq": 3 - mz}, device_id_type=MESH)
-
-    pl.semaphore_wait(barrier, nx + 1 + is_inner.astype(jnp.int32))
 
     def x_copy(d, k, piece):
         here = down.at[k, :, pl.ds(piece * fl, fl)]
@@ -572,27 +585,41 @@
             device_id={"freq": to}, device_id_type=MESH,
         )
 
-    def chunk_copy(kind, slot, k, lo, count, to):
-        row = pl.multiple_of(slot * part + k * n, n)
-        here = spec.at[pl.ds(lo, count), pl.ds(row, n)]
+    def chunk_copy(kind, slot, k, count, to):
+        here = spec.at[slot * nchunk + k, pl.ds(0, count)]
         return z_copy(kind, k, here, here, to)
 
     def block_copy(kind, slot, b, to):
-        here = spec.at[b, pl.ds(pl.multiple_of(slot * part, part), part)]
+        here = spec.at[pl.ds(slot * nchunk, nchunk), b]
         return z_copy(kind, b, here, here, to)
 
-    late = blocks - early
-    to_inner_early = lambda k: chunk_copy(0, end, k, 0, early, inner)
-    to_inner_late = lambda k: chunk_copy(1, end, k, early, late, inner)
-    across_own = lambda k, own: chunk_copy(2, own, k, 0, early, 3 - mz)
-    across_end = lambda k, of: chunk_copy(3, of, k, 0, early, 3 - mz)
-    out_own = lambda k: chunk_copy(4, inner, k, 0, plain, end)
-    out_opp = lambda k: chunk_copy(5, 3 - inner, k, 0, plain, end)
-    out_far = lambda k: chunk_copy(6, 3 - end, k, 0, plain, end)
-    block_own = lambda b, own: block_copy(7, own, b, 3 - mz)
-    block_end = lambda b, of: block_copy(8, of, b, 3 - mz)
-    trace_copy = lambda b: z_copy(9, b, made.at[b - plain], out.at[b], end)
-
+    end_near = lambda k: chunk_copy(0, end, k, early, inner)
+    end_far = lambda k, of: chunk_copy(1, of, k, early, 3 - inner)
+    across = lambda k, own: chunk_copy(2, own, k, early, 3 - mz)
+
+    def outward(kind, slot, k, act):
+        @pl.when(wide)
+        def _():
+            act(chunk_copy(kind, slot, k, plain + 1, end))
+
+        @pl.when(jnp.logical_not(wide))
+        def _():
+            act(chunk_copy(kind, slot, k, plain, end))
+
+    out_own = lambda k, act: outward(3, inner, k, act)
+    out_opp = lambda k, act: outward(4, 3 - inner, k, act)
+    out_far = lambda k, act: outward(5, 3 - end, k, act)
+    start = lambda copy: copy.start()
+    wait_recv = lambda copy: copy.wait_recv()
+    wait_send = lambda copy: copy.wait_send()
+    late_near = lambda b: block_copy(6, end, b, inner)
+    late_far = lambda b, of: block_copy(7, of, b, 3 - inner)
+    late_across = lambda b, own: block_copy(8, own, b, 3 - mz)
+    trace_copy = lambda b, at: z_copy(9, b, made.at[at], out.at[b], end)
+
+    for copy in smalls:
+        copy.wait()
+    level = thr[0].astype(jnp.float32) / 64.0
     line, column = iota((lines, width), 0), mc * width + iota((lines, width), 1)
     select = jnp.zeros((lines, width), jnp.float32)
     for s in range(lines):
@@ -609,6 +636,8 @@
             down[k, c, pl.ds(pl.multiple_of(mx * fl, fl), fl)] = jnp.concatenate(
                 parts, axis=0
             ).astype(jnp.bfloat16)
+
+    def share_down(k):
         for d in range(1, nx):
             x_copy(d, k, mx).start()
 
@@ -680,41 +709,47 @@
         grad = jnp.dot(e, down[k].reshape(2 * cols, width), preferred_element_type=jnp.float32)
         new = (spectra_of(k).astype(jnp.float32) - scale * (grad * norm)).astype(jnp.bfloat16)
         new = jnp.dot(perm, new, preferred_element_type=jnp.float32).astype(jnp.bfloat16)
-        row = pl.multiple_of(mz * part + k * n, n)
         for b in range(blocks):
-            spec[b, pl.ds(row, n)] = new[:, b * BLOCK:(b + 1) * BLOCK]
+            spec[mz * nchunk + k, b] = new[:, b * TILE:(b + 1) * TILE]
 
     def send(k):
         @pl.when(is_end)
         def _():
-            to_inner_early(k).start()
-            to_inner_late(k).start()
+            end_far(k, mz).start()
+            end_near(k).start()
 
         @pl.when(is_inner)
         def _():
-            across_own(k, mz).start()
-            out_own(k).start()
+            out_own(k, start)
+            across(k, mz).start()
 
     def relay(k):
-        @pl.when(is_inner & (k >= 1) & (k <= nchunk))
+        across(k, 3 - mz).wait_recv()
+        out_opp(k, start)
+        end_far(k, 3 - end).wait_recv()
+        out_far(k, start)
+
+    make_down(0)
+    pl.semaphore_wait(barrier, nx + 2 + is_inner.astype(jnp.int32))
+    share_down(0)
+
+    def load_all(k, carry):
+        @pl.when(k > 0)
         def _():
-            to_inner_early(k - 1).wait_recv()
-            across_end(k - 1, end).start()
-            across_own(k - 1, 3 - mz).wait_recv()
-            out_opp(k - 1).start()
-
-        @pl.when(is_inner & (k >= 2))
-        def _():
-            across_end(k - 2, 3 - end).wait_recv()
-            out_far(k - 2).start()
-
-    make_down(0)
+            load(data, dbuf, d_sem, k).start()
+
+        load(est, ebuf, e_sem, k).start()
+        return carry
+
+    lax.fori_loop(0, nchunk, load_all, 0)
     make_down(1)
+    share_down(1)
 
     def step_of(k, carry):
         @pl.when(k < nchunk - 2)
         def _():
             make_down(k + 2)
+            share_down(k + 2)
 
         for j, z in enumerate((mz, end)):
             @pl.when(k == nchunk // 4 * (j + 1))
@@ -727,23 +762,24 @@
             update(k)
             send(k)
 
-        relay(k)
+        @pl.when(is_inner & (k >= 1))
+        def _():
+            relay(k - 1)
+
         return carry
 
-    lax.fori_loop(0, nchunk + 2, step_of, 0)
-
-    def traces(b, table, to):
-        make_pairs(
-            spec.at[b].reshape(nz * nchunk, n, BLOCK), table, level, gain, rows, t_group,
-            sparse, to,
-        )
-
-    def own_block(b):
-        traces(b, tables.at[0], out.at[b])
-
-    def help_block(b):
-        traces(b, tables.at[1], made.at[b - plain])
-        trace_copy(b).start()
+    lax.fori_loop(0, nchunk + 1, step_of, 0)
+
+    def own_pair(b):
+        make_pairs(spec, b, tables.at[0], level, gain, rows, t_group, sparse, out, b)
+
+    def help_pair(b, at):
+        make_pairs(spec, b, tables.at[1], level, gain, rows, t_group, sparse, made, at)
+
+    def arrived(b):
+        late_near(b).wait_recv()
+        late_far(b, 3 - end).wait_recv()
+        late_across(b, 3 - mz).wait_recv()
 
     def loop(lo, hi, f):
         def one(i, carry):
@@ -754,57 +790,71 @@
 
     @pl.when(is_inner)
     def _():
-        loop(0, nchunk, lambda k: to_inner_late(k).wait_recv())
-
-        def hand_on(b):
-            block_own(b, mz).start()
-            block_end(b, end).start()
-
-        loop(early, blocks, hand_on)
-
-        loop(plain, early, help_block)
-        loop(0, early, own_block)
-
-        def rest(b):
-            block_own(b, 3 - mz).wait_recv()
-            block_end(b, 3 - end).wait_recv()
-            help_block(b)
-            own_block(b)
-
-        loop(early, blocks, rest)
+        loop(early, blocks, lambda b: late_across(b, mz).start())
+        loop(0, nchunk, lambda k: end_near(k).wait_recv())
+        narrow = 1 - wide.astype(jnp.int32)
+
+        def both(j):
+            b = first + 2 * j
+            at = jnp.minimum(b, blocks - 2)
+
+            @pl.when(b >= early)
+            def _():
+                arrived(b)
+
+            @pl.when((b + 1 >= early) & (b + 1 < blocks))
+            def _():
+                arrived(b + 1)
+
+            help_pair(at, 2 * j)
+
+            @pl.when(at == b)
+            def _():
+                trace_copy(b, 2 * j).start()
+
+            trace_copy(at + 1, 2 * j + 1).start()
+            done = (b - narrow) // 2
+            loop(jnp.where(j == 0, 0, done), done + 1, lambda i: own_pair(2 * i))
+
+        loop(0, (blocks - plain) // 2 + narrow, both)
 
         def drain(k):
-            across_own(k, mz).wait_send()
-            across_end(k, end).wait_send()
-            out_own(k).wait_send()
-            out_opp(k).wait_send()
-            out_far(k).wait_send()
+            across(k, mz).wait_send()
+            out_own(k, wait_send)
+            out_opp(k, wait_send)
+            out_far(k, wait_send)
 
         loop(0, nchunk, drain)
-
-        def drain_block(b):
-            block_own(b, mz).wait_send()
-            block_end(b, end).wait_send()
-
-        loop(early, blocks, drain_block)
-        loop(plain, blocks, lambda b: trace_copy(b).wait_send())
+        loop(early, blocks, lambda b: late_across(b, mz).wait_send())
+        loop(first, blocks, lambda b: trace_copy(b, 0).wait_send())
 
     @pl.when(is_end)
     def _():
-        def arrived(k):
-            out_own(k).wait_recv()
-            out_opp(k).wait_recv()
-            out_far(k).wait_recv()
-
-        loop(0, nchunk, arrived)
-        loop(0, plain, own_block)
-        loop(plain, blocks, lambda b: trace_copy(b).wait_recv())
+        def late(b):
+            late_far(b, mz).start()
+            late_near(b).start()
+
+        loop(early, blocks, late)
+
+        def come(k):
+            out_own(k, wait_recv)
+            out_opp(k, wait_recv)
+            out_far(k, wait_recv)
+
+        loop(0, nchunk, come)
+        loop(0, (plain + 1) // 2, lambda j: own_pair(jnp.minimum(2 * j, first - 2)))
+        loop(first, blocks, lambda b: trace_copy(b, 0).wait_recv())
 
         def drain(k):
-            to_inner_early(k).wait_send()
-            to_inner_late(k).wait_send()
+            end_near(k).wait_send()
+            end_far(k, mz).wait_send()
+
+        def drain_late(b):
+            late_near(b).wait_send()
+            late_far(b, mz).wait_send()
 
         loop(0, nchunk, drain)
+        loop(early, blocks, drain_late)
 
     def drain(k):
         for d in range(1, nx):
@@ -817,7 +867,7 @@
 def place_kernel(traces, out, sem):
     copies = [
         pltpu.make_async_copy(
-            traces.at[b], out.at[:, pl.ds(b * BLOCK, BLOCK)], sem.at[b]
+            traces.at[b], out.at[:, pl.ds(b * TILE, TILE)], sem.at[b]
         )
         for b in range(traces.shape[0])
     ]
@@ -836,12 +886,12 @@
     fi, cols = GF * rows, nx * GF * lines
     size = nz * nf
     nt = NT // nz
-    blocks = width // BLOCK
-    plain, early = 3 * blocks // 8, blocks // 2
+    blocks = width // TILE
+    plain = PLAIN * blocks // 16
+    early = plain + 3
     gain, t_group = math.sqrt(RCV / NF), 32
 
     vmem = pl.BlockSpec(memory_space=pltpu.VMEM)
-    smem = pl.BlockSpec(memory_space=pltpu.SMEM)
     hbm = pl.BlockSpec(memory_space=pl.ANY)
     dma = pltpu.SemaphoreType.DMA
     traces = pl.pallas_call(
@@ -849,19 +899,26 @@
             relay_kernel, nx, nz, nchunk, rows, lines, shots, norm, blocks, plain, early,
             gain, t_group,
         ),
-        out_shape=pltpu.VMEM((blocks, nt * rows, BLOCK), jnp.bfloat16),
-        in_specs=[hbm, hbm, vmem, smem, smem, vmem, smem, smem],
+        out_shape=pltpu.VMEM((blocks, nt * rows, TILE), jnp.bfloat16),
+        in_specs=[hbm] * 8,
         out_specs=vmem,
         scratch_shapes=[
+            pltpu.VMEM((2 * rows * shots, nf), jnp.bfloat16),
+            pltpu.SMEM((2, nf), jnp.float32),
+            pltpu.SMEM((lines,), jnp.int32),
+            pltpu.VMEM((1, size), jnp.int32),
+            pltpu.SMEM((1,), jnp.int32),
+            pltpu.SMEM((1,), jnp.float32),
+            dma((6,)),
             pltpu.VMEM((nchunk, 2, GF * lines, width), jnp.bfloat16),
             pltpu.VMEM((nchunk, 2, fi, width), jnp.bfloat16),
             pltpu.VMEM((nchunk, 2, cols, width), jnp.bfloat16),
-            pltpu.VMEM((blocks, nz * nchunk * 2 * fi, BLOCK), jnp.bfloat16),
+            pltpu.VMEM((nz * nchunk, blocks, 2 * fi, TILE), jnp.bfloat16),
             pltpu.VMEM((nchunk, 2, fi, cols), jnp.float32),
             pltpu.VMEM((nchunk, 2, fi, cols), jnp.float32),
             pltpu.VMEM((2, PAIR * nt, 2 * PAIR * size), jnp.bfloat16),
-            pltpu.VMEM((rows // PAIR, PAIR * nt, BLOCK), jnp.bfloat16),
-            pltpu.VMEM((blocks - plain, nt * rows, BLOCK), jnp.bfloat16),
+            pltpu.VMEM((rows // PAIR, PAIR * nt, 2 * TILE), jnp.bfloat16),
+            pltpu.VMEM((blocks - plain + 1, nt * rows, TILE), jnp.bfloat16),
             dma((nchunk,)), dma((nchunk,)),
             dma((nx, nchunk)), dma((nx, nchunk)),
             dma((nchunk,)), dma((nchunk,)),

time: 244 us -> 240 us (0.984)
  Pallas kernels: 242 us -> 238 us
    pallas_call x1, Pallas kernels: 239 us -> 235 us  [relay_body(): pl.pallas_call(partial(relay_kernel, nx, nz, nchunk, rows, lines, shots,...]
where the time goes in v3:
time: 240 us
  Pallas kernels  238 us (99%)
    pallas_call x1, Pallas kernels, relay_body(): pl.pallas_call(partial(relay_kernel, nx, nz, nchunk, rows, lines, shots,...  235 us

profile of v3, /device:TPU:1, one launch (start us, length us, event | category | flops | bytes accessed | tf_op | source)
XLA Modules:
  0.0 239.7 jit_solution(13665804288390413625)
XLA Ops:
  1.3 235.0 %relay.1.traces = bf16[16,2048,128]{2,1,0:T(8,128)(2,1)S(1)} custom-call(bf16[2,512,2048]{2,1,0:T(8,128)(2,1)} %bitcast.7, bf16[2,512,2048]{2,1,0:T(8,128)(2,1)} %bitcast.8, bf16[256,64]{1,0:T(8,128)(2,1)} %bitcast.9, f32[2,64]{1,0:T(2,128)} %wav_in.1, s32[8]{0:T(128)} %pos_in.1, s32[1,256]{1,0:T(1,128)} %bitcast.10, s32[1]{0:T(128)S(6)} %copy.9.thr_in, ...), custom_call_target="tpu_custom_call" | custom-call | tf_op jit(solution)/shard_map/relay/pallas_call | solution.py:897
  236.3 3.4 %place.1 = bf16[2048,2048]{1,0:T(8,128)(2,1)} custom-call(bf16[16,2048,128]{2,1,0:T(8,128)(2,1)S(1)} %relay.1.traces), custom_call_target="tpu_custom_call" | custom-call | tf_op jit(solution)/shard_map/place/pallas_call | solution.py:941

commit v4 on v3

--- a/solution.py
+++ b/solution.py
@@ -16,6 +16,7 @@
 PAIR = 2
 TILE = 128
 PLAIN = 5
+AHEAD = 4
 BLOCK = 256
 LAG = 1
 MESH = pl.DeviceIdType.MESH
@@ -515,7 +516,8 @@
     data, est, win_in, wav_in, pos_in, bins_in, thr_in, step_in, out,
     win, wav, pos, bins, thr, step, i_sem,
     dbuf, ebuf, down, spec, mod_mine, mod_other, tables, sparse, made,
-    d_sem, e_sem, x_send, x_recv, c_send, c_recv, z_send, z_recv,
+    d_sem, e_sem, x_send, x_recv, c_send, c_recv, z_send, near_recv, far_recv, across_recv,
+    out_recv, late_recv, trace_recv,
 ):
     mx = lax.axis_index("shot")
     mz = lax.axis_index("freq")
@@ -541,12 +543,13 @@
 
     def load(ref, buf, sem, k):
         return pltpu.make_async_copy(
-            ref.at[:, pl.ds(pl.multiple_of(k * fl, fl), fl)], buf.at[k], sem.at[k]
+            ref.at[:, pl.ds(pl.multiple_of(k * fl, fl), fl)], buf.at[k], sem.at[k % AHEAD]
         )
 
     for copy in smalls[:2]:
         copy.start()
-    load(data, dbuf, d_sem, 0).start()
+    for k in range(AHEAD):
+        load(data, dbuf, d_sem, k).start()
     for copy in smalls[2:]:
         copy.start()
 
@@ -564,47 +567,70 @@
         pl.semaphore_signal(barrier, inc=1, device_id={"freq": 3 - mz}, device_id_type=MESH)
 
     def x_copy(d, k, piece):
-        here = down.at[k, :, pl.ds(piece * fl, fl)]
+        here = down.at[k, :, pl.ds(piece * fl, fl)] if k is not None else (
+            down.at[:, :, pl.ds(piece * fl, fl)]
+        )
         return pltpu.make_async_remote_copy(
             src_ref=here, dst_ref=here,
-            send_sem=x_send.at[d, k], recv_sem=x_recv.at[d, k],
+            send_sem=x_send.at[d - 1], recv_sem=x_recv.at[d - 1, 0 if k is None else k],
             device_id={"shot": lax.rem(mx + d, nx)}, device_id_type=MESH,
         )
 
     def c_copy(k):
         return pltpu.make_async_remote_copy(
             src_ref=mod_mine.at[k], dst_ref=mod_other.at[k],
-            send_sem=c_send.at[k], recv_sem=c_recv.at[k],
+            send_sem=c_send.at[0], recv_sem=c_recv.at[k % 2],
             device_id={"rcv": 1 - mc}, device_id_type=MESH,
         )
 
-    def z_copy(kind, at, here, there, to):
+    c_all = pltpu.make_async_remote_copy(
+        src_ref=mod_mine, dst_ref=mod_other, send_sem=c_send.at[0], recv_sem=c_recv.at[0],
+        device_id={"rcv": 1 - mc}, device_id_type=MESH,
+    )
+
+    def z_copy(kind, here, there, recv, to):
         return pltpu.make_async_remote_copy(
-            src_ref=here, dst_ref=there,
-            send_sem=z_send.at[kind, at], recv_sem=z_recv.at[kind, at],
+            src_ref=here, dst_ref=there, send_sem=z_send.at[kind], recv_sem=recv,
             device_id={"freq": to}, device_id_type=MESH,
         )
 
-    def chunk_copy(kind, slot, k, count, to):
-        here = spec.at[slot * nchunk + k, pl.ds(0, count)]
-        return z_copy(kind, k, here, here, to)
+    def chunk_copy(kind, slot, k, count, recv, to):
+        at = slot * nchunk + k if k is not None else pl.ds(slot * nchunk, nchunk)
+        here = spec.at[at, pl.ds(0, count)]
+        return z_copy(kind, here, here, recv, to)
 
     def block_copy(kind, slot, b, to):
-        here = spec.at[pl.ds(slot * nchunk, nchunk), b]
-        return z_copy(kind, b, here, here, to)
-
-    end_near = lambda k: chunk_copy(0, end, k, early, inner)
-    end_far = lambda k, of: chunk_copy(1, of, k, early, 3 - inner)
-    across = lambda k, own: chunk_copy(2, own, k, early, 3 - mz)
+        at = b if b is not None else pl.ds(early, blocks - early)
+        here = spec.at[pl.ds(slot * nchunk, nchunk), at]
+        recv = late_recv.at[kind - 6, b - early if b is not None else 0]
+        return z_copy(kind, here, here, recv, to)
+
+    which = lambda k: 0 if k is None else k
+    end_near = lambda k: chunk_copy(0, end, k, early, near_recv.at[0], inner)
+    end_far = lambda k, of: chunk_copy(1, of, k, early, far_recv.at[which(k)], 3 - inner)
+    across = lambda k, own: chunk_copy(2, own, k, early, across_recv.at[which(k)], 3 - mz)
+    late_near = lambda b: block_copy(6, end, b, inner)
+    late_far = lambda b, of: block_copy(7, of, b, 3 - inner)
+    late_across = lambda b, own: block_copy(8, own, b, 3 - mz)
+    trace_copy = lambda b, at: z_copy(9, made.at[at], out.at[b], trace_recv.at[0], end)
+
+    def by_core(act):
+        @pl.when(wide)
+        def _():
+            act(plain + 1)
+
+        @pl.when(jnp.logical_not(wide))
+        def _():
+            act(plain)
+
+    def traces_done(act):
+        by_core(lambda count: act(z_copy(
+            9, made.at[pl.ds(0, blocks - count)], out.at[pl.ds(0, blocks - count)], trace_recv.at[0],
+            end,
+        )))
 
     def outward(kind, slot, k, act):
-        @pl.when(wide)
-        def _():
-            act(chunk_copy(kind, slot, k, plain + 1, end))
-
-        @pl.when(jnp.logical_not(wide))
-        def _():
-            act(chunk_copy(kind, slot, k, plain, end))
+        by_core(lambda count: act(chunk_copy(kind, slot, k, count, out_recv.at[kind - 3], end)))
 
     out_own = lambda k, act: outward(3, inner, k, act)
     out_opp = lambda k, act: outward(4, 3 - inner, k, act)
@@ -612,10 +638,6 @@
     start = lambda copy: copy.start()
     wait_recv = lambda copy: copy.wait_recv()
     wait_send = lambda copy: copy.wait_send()
-    late_near = lambda b: block_copy(6, end, b, inner)
-    late_far = lambda b, of: block_copy(7, of, b, 3 - inner)
-    late_across = lambda b, own: block_copy(8, own, b, 3 - mz)
-    trace_copy = lambda b, at: z_copy(9, b, made.at[at], out.at[b], end)
 
     for copy in smalls:
         copy.wait()
@@ -627,6 +649,11 @@
 
     def make_down(k):
         load(data, dbuf, d_sem, k).wait()
+
+        @pl.when(k + AHEAD < nchunk)
+        def _():
+            load(data, dbuf, d_sem, k + AHEAD).start()
+
         for c in range(2):
             parts = []
             lines_k = dbuf[k, c].astype(jnp.float32)
@@ -681,6 +708,11 @@
 
     def model(k):
         load(est, ebuf, e_sem, k).wait()
+
+        @pl.when(k + AHEAD < nchunk)
+        def _():
+            load(est, ebuf, e_sem, k + AHEAD).start()
+
         for d in range(1, nx):
             x_copy(d, k, lax.rem(mx + nx - d, nx)).wait_recv()
         m_re, m_im = [
@@ -733,15 +765,8 @@
     pl.semaphore_wait(barrier, nx + 2 + is_inner.astype(jnp.int32))
     share_down(0)
 
-    def load_all(k, carry):
-        @pl.when(k > 0)
-        def _():
-            load(data, dbuf, d_sem, k).start()
-
+    for k in range(AHEAD):
         load(est, ebuf, e_sem, k).start()
-        return carry
-
-    lax.fori_loop(0, nchunk, load_all, 0)
     make_down(1)
     share_down(1)
 
@@ -791,42 +816,41 @@
     @pl.when(is_inner)
     def _():
         loop(early, blocks, lambda b: late_across(b, mz).start())
-        loop(0, nchunk, lambda k: end_near(k).wait_recv())
+        end_near(None).wait_recv()
         narrow = 1 - wide.astype(jnp.int32)
 
         def both(j):
             b = first + 2 * j
-            at = jnp.minimum(b, blocks - 2)
 
             @pl.when(b >= early)
             def _():
                 arrived(b)
 
-            @pl.when((b + 1 >= early) & (b + 1 < blocks))
+            @pl.when(b + 1 >= early)
             def _():
                 arrived(b + 1)
 
-            help_pair(at, 2 * j)
-
-            @pl.when(at == b)
-            def _():
-                trace_copy(b, 2 * j).start()
-
-            trace_copy(at + 1, 2 * j + 1).start()
+            help_pair(b, 2 * j)
+            trace_copy(b, 2 * j).start()
+            trace_copy(b + 1, 2 * j + 1).start()
             done = (b - narrow) // 2
             loop(jnp.where(j == 0, 0, done), done + 1, lambda i: own_pair(2 * i))
 
-        loop(0, (blocks - plain) // 2 + narrow, both)
-
-        def drain(k):
-            across(k, mz).wait_send()
-            out_own(k, wait_send)
-            out_opp(k, wait_send)
-            out_far(k, wait_send)
-
-        loop(0, nchunk, drain)
-        loop(early, blocks, lambda b: late_across(b, mz).wait_send())
-        loop(first, blocks, lambda b: trace_copy(b, 0).wait_send())
+        loop(0, (blocks - plain) // 2, both)
+
+        @pl.when(jnp.logical_not(wide))
+        def _():
+            last = blocks - 1
+            arrived(last)
+            help_pair(last - 1, last - plain)
+            trace_copy(last, last - plain + 1).start()
+            own_pair(last - 1)
+
+        across(None, mz).wait_send()
+        late_across(None, mz).wait_send()
+        for copies in (out_own, out_opp, out_far):
+            copies(None, wait_send)
+        traces_done(wait_send)
 
     @pl.when(is_end)
     def _():
@@ -836,32 +860,18 @@
 
         loop(early, blocks, late)
 
-        def come(k):
-            out_own(k, wait_recv)
-            out_opp(k, wait_recv)
-            out_far(k, wait_recv)
-
-        loop(0, nchunk, come)
+        for copies in (out_own, out_opp, out_far):
+            copies(None, wait_recv)
         loop(0, (plain + 1) // 2, lambda j: own_pair(jnp.minimum(2 * j, first - 2)))
-        loop(first, blocks, lambda b: trace_copy(b, 0).wait_recv())
-
-        def drain(k):
-            end_near(k).wait_send()
-            end_far(k, mz).wait_send()
-
-        def drain_late(b):
-            late_near(b).wait_send()
-            late_far(b, mz).wait_send()
-
-        loop(0, nchunk, drain)
-        loop(early, blocks, drain_late)
-
-    def drain(k):
-        for d in range(1, nx):
-            x_copy(d, k, mx).wait_send()
-        c_copy(k).wait_send()
-
-    loop(0, nchunk, drain)
+        traces_done(wait_recv)
+        end_near(None).wait_send()
+        end_far(None, mz).wait_send()
+        late_near(None).wait_send()
+        late_far(None, mz).wait_send()
+
+    for d in range(1, nx):
+        x_copy(d, None, mx).wait_send()
+    c_all.wait_send()
 
 
 def place_kernel(traces, out, sem):
@@ -919,10 +929,11 @@
             pltpu.VMEM((2, PAIR * nt, 2 * PAIR * size), jnp.bfloat16),
             pltpu.VMEM((rows // PAIR, PAIR * nt, 2 * TILE), jnp.bfloat16),
             pltpu.VMEM((blocks - plain + 1, nt * rows, TILE), jnp.bfloat16),
-            dma((nchunk,)), dma((nchunk,)),
-            dma((nx, nchunk)), dma((nx, nchunk)),
-            dma((nchunk,)), dma((nchunk,)),
-            dma((10, max(nchunk, blocks))), dma((10, max(nchunk, blocks))),
+            dma((AHEAD,)), dma((AHEAD,)),
+            dma((nx - 1,)), dma((nx - 1, nchunk)),
+            dma((1,)), dma((2,)),
+            dma((10,)), dma((1,)), dma((nchunk,)), dma((nchunk,)),
+            dma((3,)), dma((3, blocks - early)), dma((1,)),
         ],
         compiler_params=pltpu.CompilerParams(
             collective_id=1, has_side_effects=True, vmem_limit_bytes=48 << 20

time: 240 us -> 236 us (0.983)
  Pallas kernels: 238 us -> 235 us
    pallas_call x1, Pallas kernels: 235 us -> 232 us  [relay_body(): pl.pallas_call(partial(relay_kernel, nx, nz, nchunk, rows, lines, shots,...]
where the time goes in v4:
time: 236 us
  Pallas kernels  235 us (100%)
    pallas_call x1, Pallas kernels, relay_body(): pl.pallas_call(partial(relay_kernel, nx, nz, nchunk, rows, lines, shots,...  232 us

profile of v4, /device:TPU:1, one launch (start us, length us, event | category | flops | bytes accessed | tf_op | source)
XLA Modules:
  0.0 236.3 jit_solution(16198623586022474727)
XLA Ops:
  1.3 231.6 %relay.1.traces = bf16[16,2048,128]{2,1,0:T(8,128)(2,1)S(1)} custom-call(bf16[2,512,2048]{2,1,0:T(8,128)(2,1)} %bitcast.7, bf16[2,512,2048]{2,1,0:T(8,128)(2,1)} %bitcast.8, bf16[256,64]{1,0:T(8,128)(2,1)} %bitcast.9, f32[2,64]{1,0:T(2,128)} %wav_in.1, s32[8]{0:T(128)} %pos_in.1, s32[1,256]{1,0:T(1,128)} %bitcast.10, s32[1]{0:T(128)S(6)} %copy.9.thr_in, ...), custom_call_target="tpu_custom_call" | custom-call | tf_op jit(solution)/shard_map/relay/pallas_call | solution.py:907
  232.9 3.4 %place.1 = bf16[2048,2048]{1,0:T(8,128)(2,1)} custom-call(bf16[16,2048,128]{2,1,0:T(8,128)(2,1)S(1)} %relay.1.traces), custom_call_target="tpu_custom_call" | custom-call | tf_op jit(solution)/shard_map/place/pallas_call | solution.py:952

commit v5 on v4

--- a/solution.py
+++ b/solution.py
@@ -516,7 +516,7 @@
     data, est, win_in, wav_in, pos_in, bins_in, thr_in, step_in, out,
     win, wav, pos, bins, thr, step, i_sem,
     dbuf, ebuf, down, spec, mod_mine, mod_other, tables, sparse, made,
-    d_sem, e_sem, x_send, x_recv, c_send, c_recv, z_send, near_recv, far_recv, across_recv,
+    d_sem, e_sem, x_send, x_recv, c_send, c_recv, z_send, near_recv, pair_recv,
     out_recv, late_recv, trace_recv,
 ):
     mx = lax.axis_index("shot")
@@ -602,13 +602,13 @@
     def block_copy(kind, slot, b, to):
         at = b if b is not None else pl.ds(early, blocks - early)
         here = spec.at[pl.ds(slot * nchunk, nchunk), at]
-        recv = late_recv.at[kind - 6, b - early if b is not None else 0]
+        recv = late_recv.at[b - early if b is not None else 0]
         return z_copy(kind, here, here, recv, to)
 
     which = lambda k: 0 if k is None else k
     end_near = lambda k: chunk_copy(0, end, k, early, near_recv.at[0], inner)
-    end_far = lambda k, of: chunk_copy(1, of, k, early, far_recv.at[which(k)], 3 - inner)
-    across = lambda k, own: chunk_copy(2, own, k, early, across_recv.at[which(k)], 3 - mz)
+    end_far = lambda k, of: chunk_copy(1, of, k, early, pair_recv.at[which(k)], 3 - inner)
+    across = lambda k, own: chunk_copy(2, own, k, early, pair_recv.at[which(k)], 3 - mz)
     late_near = lambda b: block_copy(6, end, b, inner)
     late_far = lambda b, of: block_copy(7, of, b, 3 - inner)
     late_across = lambda b, own: block_copy(8, own, b, 3 - mz)
@@ -756,9 +756,9 @@
             across(k, mz).start()
 
     def relay(k):
-        across(k, 3 - mz).wait_recv()
+        two = spec.at[pl.ds(0, 2), pl.ds(0, early)]
+        z_copy(2, two, two, pair_recv.at[k], 3 - mz).wait_recv()
         out_opp(k, start)
-        end_far(k, 3 - end).wait_recv()
         out_far(k, start)
 
     make_down(0)
@@ -802,9 +802,8 @@
         make_pairs(spec, b, tables.at[1], level, gain, rows, t_group, sparse, made, at)
 
     def arrived(b):
-        late_near(b).wait_recv()
-        late_far(b, 3 - end).wait_recv()
-        late_across(b, 3 - mz).wait_recv()
+        three = spec.at[pl.ds(0, nchunk), pl.ds(0, 3)]
+        z_copy(8, three, three, late_recv.at[b - early], 3 - mz).wait_recv()
 
     def loop(lo, hi, f):
         def one(i, carry):
@@ -932,8 +931,8 @@
             dma((AHEAD,)), dma((AHEAD,)),
             dma((nx - 1,)), dma((nx - 1, nchunk)),
             dma((1,)), dma((2,)),
-            dma((10,)), dma((1,)), dma((nchunk,)), dma((nchunk,)),
-            dma((3,)), dma((3, blocks - early)), dma((1,)),
+            dma((10,)), dma((1,)), dma((nchunk,)),
+            dma((3,)), dma((blocks - early,)), dma((1,)),
         ],
         compiler_params=pltpu.CompilerParams(
             collective_id=1, has_side_effects=True, vmem_limit_bytes=48 << 20

time: 236 us -> 236 us (level)
  no operation moved by 1% of the time
where the time goes in v5:
time: 236 us
  Pallas kernels  235 us (100%)
    pallas_call x1, Pallas kernels, relay_body(): pl.pallas_call(partial(relay_kernel, nx, nz, nchunk, rows, lines, shots,...  231 us

profile of v5, /device:TPU:1, one launch (start us, length us, event | category | flops | bytes accessed | tf_op | source)
XLA Modules:
  0.0 236.0 jit_solution(11431416535810347807)
XLA Ops:
  1.3 231.3 %relay.1.traces = bf16[16,2048,128]{2,1,0:T(8,128)(2,1)S(1)} custom-call(bf16[2,512,2048]{2,1,0:T(8,128)(2,1)} %bitcast.7, bf16[2,512,2048]{2,1,0:T(8,128)(2,1)} %bitcast.8, bf16[256,64]{1,0:T(8,128)(2,1)} %bitcast.9, f32[2,64]{1,0:T(2,128)} %wav_in.1, s32[8]{0:T(128)} %pos_in.1, s32[1,256]{1,0:T(1,128)} %bitcast.10, s32[1]{0:T(128)S(6)} %copy.9.thr_in, ...), custom_call_target="tpu_custom_call" | custom-call | tf_op jit(solution)/shard_map/relay/pallas_call | solution.py:906
  232.6 3.4 %place.1 = bf16[2048,2048]{1,0:T(8,128)(2,1)} custom-call(bf16[16,2048,128]{2,1,0:T(8,128)(2,1)S(1)} %relay.1.traces), custom_call_target="tpu_custom_call" | custom-call | tf_op jit(solution)/shard_map/place/pallas_call | solution.py:951

commit v6 on v5

--- a/solution.py
+++ b/solution.py
@@ -738,11 +738,20 @@
         e = jnp.concatenate(
             [jnp.concatenate([e_re, e_im], axis=1), jnp.concatenate([e_im, -e_re], axis=1)], axis=0
         ).astype(jnp.bfloat16)
-        grad = jnp.dot(e, down[k].reshape(2 * cols, width), preferred_element_type=jnp.float32)
-        new = (spectra_of(k).astype(jnp.float32) - scale * (grad * norm)).astype(jnp.bfloat16)
-        new = jnp.dot(perm, new, preferred_element_type=jnp.float32).astype(jnp.bfloat16)
-        for b in range(blocks):
-            spec[mz * nchunk + k, b] = new[:, b * TILE:(b + 1) * TILE]
+        for lo, hi in ((0, early), (early, blocks)):
+            at = slice(lo * TILE, hi * TILE)
+            wide_part = (hi - lo) * TILE
+            grad = jnp.dot(
+                e, down[k, :, :, at].reshape(2 * cols, wide_part),
+                preferred_element_type=jnp.float32,
+            )
+            old = ebuf[k, :, :, at].reshape(n, wide_part)
+            new = (old.astype(jnp.float32) - scale * (grad * norm)).astype(jnp.bfloat16)
+            new = jnp.dot(perm, new, preferred_element_type=jnp.float32).astype(jnp.bfloat16)
+            for b in range(lo, hi):
+                spec[mz * nchunk + k, b] = new[:, (b - lo) * TILE:(b - lo + 1) * TILE]
+            if lo == 0:
+                send(k)
 
     def send(k):
         @pl.when(is_end)
@@ -785,7 +794,6 @@
         def _():
             model(k)
             update(k)
-            send(k)
 
         @pl.when(is_inner & (k >= 1))
         def _():

time: 236 us -> 236 us (level)
  no operation moved by 1% of the time
where the time goes in v6:
time: 236 us
  Pallas kernels  235 us (100%)
    pallas_call x1, Pallas kernels, relay_body(): pl.pallas_call(partial(relay_kernel, nx, nz, nchunk, rows, lines, shots,...  231 us

profile of v6, /device:TPU:1, one launch (start us, length us, event | category | flops | bytes accessed | tf_op | source)
XLA Modules:
  0.0 236.0 jit_solution(9432584005723350433)
XLA Ops:
  1.3 231.2 %relay.1.traces = bf16[16,2048,128]{2,1,0:T(8,128)(2,1)S(1)} custom-call(bf16[2,512,2048]{2,1,0:T(8,128)(2,1)} %bitcast.7, bf16[2,512,2048]{2,1,0:T(8,128)(2,1)} %bitcast.8, bf16[256,64]{1,0:T(8,128)(2,1)} %bitcast.9, f32[2,64]{1,0:T(2,128)} %wav_in.1, s32[8]{0:T(128)} %pos_in.1, s32[1,256]{1,0:T(1,128)} %bitcast.10, s32[1]{0:T(128)S(6)} %copy.9.thr_in, ...), custom_call_target="tpu_custom_call" | custom-call | tf_op jit(solution)/shard_map/relay/pallas_call | solution.py:914
  232.5 3.4 %place.1 = bf16[2048,2048]{1,0:T(8,128)(2,1)} custom-call(bf16[16,2048,128]{2,1,0:T(8,128)(2,1)S(1)} %relay.1.traces), custom_call_target="tpu_custom_call" | custom-call | tf_op jit(solution)/shard_map/place/pallas_call | solution.py:959
